TPU v7x, 32 devices: a whole 2x2x4 slice. The times are simulated.
32 devices in a mesh: grp: 4 (over x, core), dev: 8 (over z, y).
Axes of the slice: x: 2, y: 2, z: 4, core: 2. Of those that a mesh axis runs over, the one named last changes fastest.
Arguments:
- density: float32 [2, 8192, 8192], P(None, 'dev', 'grp'), may hold values from -64 to 64, as said below
- costate: float32 [2, 8192, 8192], P(None, 'dev', 'grp'), may hold values from -64 to 64, as said below
- phases: float32 [24, 2, 64], replicated, may hold values from -3.140625 to 3.140625
- displacements: float32 [24, 2, 2, 64, 64], replicated, may hold values from -0.5 to 0.5
- table_slot: int32 [24], replicated, may hold values from 0 to 23, each once
- checkpoint: int32 [1], replicated, may hold values from 0 to 22
Outputs:
- costate_start: float32 [2, 8192, 8192], P(None, 'dev', 'grp')
- phase_grads: float32 [2, 2, 64], replicated
Inputs may be any that keep to these rules, and one draw needn't show every extreme that they name: `density`: Hermitian: real part symmetric, imaginary part antisymmetric. `costate`: Hermitian: real part symmetric, imaginary part antisymmetric. `table_slot`: every row of phases once.
All inputs are finite; a program needn't handle non-finite values.
Results may differ from a plain program's by a relative error of at most 0.00011.
Values sent between devices are 32-bit elements; how exact they have to be, the bound alone decides.
No kernel may reach another device: no remote copies, remote signals or barrier semaphores. Data moves between devices by JAX's collectives and lax.ppermute only.
A program may use at most 384 MiB of HBM per device.

v0:
```python
import functools

import jax
import jax.numpy as jnp
from jax import lax
from jax.experimental import pallas as pl
from jax.experimental.pallas import tpu as pltpu
from jax.sharding import PartitionSpec as P

LEVELS = 64
TRANSMON = 2
WIDE = LEVELS * TRANSMON
PAIR = 2 * WIDE
HIGH = lax.Precision.HIGHEST
F32 = jnp.float32
BF16 = jnp.bfloat16
SMALL = pl.CostEstimate(flops=1024, bytes_accessed=1024, transcendentals=0)
LARGE = pl.CostEstimate(flops=2 * 10**11, bytes_accessed=1024, transcendentals=0)
PARAMS = pltpu.CompilerParams(vmem_limit_bytes=48 * 1024 * 1024)


def split_value(value):
    high = value.astype(BF16)
    low = (value - high.astype(F32)).astype(BF16)
    return high, low


def mxu(left, right, dims=(((1,), (0,)), ((), ()))):
    return lax.dot_general(left, right, dims, preferred_element_type=F32)


def exact(left, right, dims=(((1,), (0,)), ((), ()))):
    return lax.dot_general(left, right, dims, precision=HIGH, preferred_element_type=F32)


def grid_of(shape, dim):
    return lax.broadcasted_iota(jnp.int32, shape, dim)


def pick_matrix(count, chosen):
    shape = (count, count)
    return (chosen(grid_of(shape, 0)) == grid_of(shape, 1)).astype(F32)


def spread(matrix):
    tall = (grid_of((WIDE, LEVELS), 0) // TRANSMON == grid_of((WIDE, LEVELS), 1)).astype(F32)
    long = (grid_of((LEVELS, WIDE), 1) // TRANSMON == grid_of((LEVELS, WIDE), 0)).astype(F32)
    same = grid_of((WIDE, WIDE), 0) % TRANSMON == grid_of((WIDE, WIDE), 1) % TRANSMON
    return jnp.where(same, exact(exact(tall, matrix), long), 0.0)


def blocks(upper_left, upper_right, lower_left, lower_right):
    return jnp.concatenate(
        [
            jnp.concatenate([upper_left, upper_right], axis=1),
            jnp.concatenate([lower_left, lower_right], axis=1),
        ],
        axis=0,
    )


def complex_product(left, right):
    return (
        exact(left[0], right[0]) - exact(left[1], right[1]),
        exact(left[0], right[1]) + exact(left[1], right[0]),
    )


def weights_kernel(parts, chunks, slot_ref, start_ref, seat_ref, *refs):
    angle_refs, matrix_refs = refs[0:2], refs[2:4]
    open_ref, turn_ref, level_ref, lane_ref = refs[-4:]
    seat = seat_ref[0]
    width = LEVELS // parts
    share = WIDE // parts
    size = share // chunks
    first, second = [], []
    for layer in range(2):
        cosine = jnp.cos(angle_refs[layer][...])
        sine = jnp.sin(angle_refs[layer][...])
        for mode, kept in enumerate((first, second)):
            turn_real, turn_imag = cosine[mode:mode + 1], sine[mode:mode + 1]
            real_part = matrix_refs[layer][mode, 0]
            imag_part = matrix_refs[layer][mode, 1]
            kept.append(
                (
                    real_part * turn_real - imag_part * turn_imag,
                    real_part * turn_imag + imag_part * turn_real,
                )
            )
    both_first = complex_product(first[1], first[0])
    both_second = complex_product(second[1], second[0])

    order = pick_matrix(
        LEVELS, lambda row: lax.bitwise_xor(row // width, seat) * width + row % width
    )

    def put_level(ref, index, real_part, imag_part):
        full = blocks(real_part, -imag_part, imag_part, real_part)
        high, low = split_value(full)
        made = blocks(high, high, low, jnp.zeros_like(low))
        if index is None:
            ref[...] = made
        else:
            ref[index] = made

    put_level(turn_ref, None, exact(both_first[0].T, order), exact(-both_first[1].T, order))
    put_level(level_ref, 0, first[1][0].T, first[1][1].T)
    put_level(level_ref, 1, exact(first[0][0], order), exact(-first[0][1], order))
    put_level(level_ref, 2, exact(order, first[0][0].T), exact(order, first[0][1].T))

    def put_lane(index, real_part, imag_part):
        real_part, imag_part = spread(real_part), spread(imag_part)
        high, low = split_value(blocks(real_part, imag_part, -imag_part, real_part))
        lane_ref[index, 0] = high
        lane_ref[index, 1] = low

    put_lane(0, *second[1])
    put_lane(1, second[0][0].T, -second[0][1].T)
    put_lane(2, *second[0])

    real_part, imag_part = spread(both_second[0].T), spread(both_second[1].T)
    full = blocks(real_part, -imag_part, -imag_part, -real_part)

    def source(row):
        chunk, rest = row // (2 * size * parts), row % (2 * size * parts)
        step, rest = rest // (2 * size), rest % (2 * size)
        half, place = rest // size, rest % size
        return half * WIDE + lax.bitwise_xor(step, seat) * share + chunk * size + place

    high, low = split_value(exact(pick_matrix(PAIR, source), full))
    open_ref[0] = high
    open_ref[1] = low


def make_weights(phases, displacements, table_slot, checkpoint, seat, parts, chunks):
    def angles(layer):
        return pl.BlockSpec(
            (None, 2, LEVELS), lambda i, slot, start, own: (slot[start[0] + layer], 0, 0)
        )

    def matrices(layer):
        return pl.BlockSpec(
            (None, 2, 2, LEVELS, LEVELS),
            lambda i, slot, start, own: (start[0] + layer, 0, 0, 0, 0),
        )

    def whole(shape):
        return pl.BlockSpec(shape, lambda i, slot, start, own: (0,) * len(shape))

    shapes = [(2, PAIR, PAIR), (PAIR, PAIR), (3, PAIR, PAIR), (3, 2, PAIR, PAIR)]
    return pl.pallas_call(
        functools.partial(weights_kernel, parts, chunks),
        grid_spec=pltpu.PrefetchScalarGridSpec(
            num_scalar_prefetch=3,
            grid=(1,),
            in_specs=[angles(0), angles(1), matrices(0), matrices(1)],
            out_specs=[whole(shape) for shape in shapes],
        ),
        out_shape=[jax.ShapeDtypeStruct(shape, BF16) for shape in shapes],
        compiler_params=PARAMS,
        cost_estimate=SMALL,
    )(table_slot, checkpoint, seat, phases, phases, displacements, displacements)


def open_kernel(count, waited, weight_ref, field_ref, *refs):
    both = jnp.concatenate([field_ref[0], field_ref[1]], axis=1)
    high, low = split_value(both)
    across = (((1,), (1,)), ((), ()))
    made = mxu(weight_ref[0], high, across) + (
        mxu(weight_ref[0], low, across) + mxu(weight_ref[1], high, across)
    )
    tall = made.shape[0] // count
    for place, out in enumerate(refs[waited:]):
        piece = made[place * tall:(place + 1) * tall]
        for first in range(out.shape[0]):
            out[first] = piece[:, first * WIDE:(first + 1) * WIDE]


def open_state(field, weights, parts, size, chunk_start, chunk_count, waited):
    rows, cols = field.shape[1:]
    firsts = rows // WIDE
    column_levels = cols // WIDE
    count = parts * chunk_count
    tall = count * 2 * size
    shape = jax.ShapeDtypeStruct((firsts, column_levels * 2 * size, WIDE), F32)
    weights = lax.slice_in_dim(
        weights, chunk_start * parts * 2 * size, chunk_start * parts * 2 * size + tall, axis=1
    )
    outs = pl.pallas_call(
        functools.partial(open_kernel, count, len(waited)),
        grid=(column_levels,),
        in_specs=[
            pl.BlockSpec((2, tall, PAIR), lambda i: (0, 0, 0)),
            pl.BlockSpec((2, rows, WIDE), lambda i: (0, 0, i)),
        ]
        + [pl.BlockSpec(memory_space=pl.ANY)] * len(waited),
        out_specs=[pl.BlockSpec((firsts, 2 * size, WIDE), lambda i: (0, i, 0))] * count,
        out_shape=[shape] * count,
        compiler_params=PARAMS,
        cost_estimate=SMALL,
    )(weights, field, *waited)
    return [outs[c * parts:(c + 1) * parts] for c in range(chunk_count)]


def cut_kernel(size, waited, seat_ref, field_ref, *refs):
    seat = seat_ref[0]
    levels = field_ref.shape[-1] // WIDE
    for step, out in enumerate(refs[waited:]):
        part = lax.bitwise_xor(seat, step)
        for half in range(2):
            for level in range(levels):
                start = (2 * level + half) * size
                out[start:start + size, :] = field_ref[
                    half, part, :, level * WIDE:(level + 1) * WIDE
                ]


def cut_pieces(field, seat, parts, chunk, size, waited):
    rows, cols = field.shape[1:]
    firsts = rows // WIDE
    chunks = WIDE // parts // size
    tall = cols // WIDE * 2 * size
    return pl.pallas_call(
        functools.partial(cut_kernel, size, len(waited)),
        grid=(firsts,),
        in_specs=[
            pl.BlockSpec(memory_space=pltpu.SMEM),
            pl.BlockSpec((2, None, parts, None, size, cols), lambda i: (0, i, 0, chunk, 0, 0)),
        ]
        + [pl.BlockSpec(memory_space=pl.ANY)] * len(waited),
        out_specs=[pl.BlockSpec((None, tall, WIDE), lambda i: (i, 0, 0))] * parts,
        out_shape=[jax.ShapeDtypeStruct((firsts, tall, WIDE), F32)] * parts,
        compiler_params=PARAMS,
        cost_estimate=SMALL,
    )(seat, field.reshape(2, firsts, parts, chunks, size, cols), *waited)


def level_apply(weights, real_part, imag_part):
    real_high, real_low = split_value(real_part)
    imag_high, imag_low = split_value(imag_part)
    stacked = jnp.concatenate([real_high, imag_high, real_low, imag_low], axis=0)
    made = mxu(weights, stacked)
    return made[:WIDE] + made[WIDE:]


def lane_apply(weight_ref, index, real_part, imag_part):
    high, low = split_value(jnp.concatenate([real_part, imag_part], axis=1))
    made = mxu(high, weight_ref[index, 0]) + (
        mxu(low, weight_ref[index, 0]) + mxu(high, weight_ref[index, 1])
    )
    return made[:, :WIDE], made[:, WIDE:]


def gather_levels(refs, size, half):
    columns = []
    for place in range(size):
        parts = [
            ref[pl.ds(half * size + place, ref.shape[0] // (2 * size), stride=2 * size), :]
            for ref in refs
        ]
        columns.append(jnp.concatenate(parts, axis=0) if len(parts) > 1 else parts[0])
    return jnp.concatenate(columns, axis=1)


def scatter_levels(ref, size, half, value):
    for place in range(size):
        ref[pl.ds(half * size + place, LEVELS, stride=2 * size), :] = value[
            :, place * WIDE:(place + 1) * WIDE
        ]


def turn_kernel(parts, size, weight_ref, *refs):
    pieces = refs[:parts]
    out_ref = refs[-1].reshape(LEVELS * 2 * size, WIDE)
    made = level_apply(
        weight_ref[...], gather_levels(pieces, size, 0), gather_levels(pieces, size, 1)
    )
    scatter_levels(out_ref, size, 0, made[:LEVELS])
    scatter_levels(out_ref, size, 1, made[LEVELS:])


def turn_columns(pieces, weights, size, waited):
    firsts = pieces[0].shape[0]
    parts = len(pieces)
    block = pieces[0].shape[1:]
    return pl.pallas_call(
        functools.partial(turn_kernel, parts, size),
        grid=(firsts,),
        in_specs=[pl.BlockSpec((PAIR, PAIR), lambda i: (0, 0))]
        + [pl.BlockSpec((None,) + block, lambda i: (i, 0, 0))] * parts
        + [pl.BlockSpec(memory_space=pl.ANY)] * len(waited),
        out_specs=pl.BlockSpec((LEVELS, None, 2 * size, WIDE), lambda i: (0, i, 0, 0)),
        out_shape=jax.ShapeDtypeStruct((LEVELS, firsts, 2 * size, WIDE), F32),
        compiler_params=PARAMS,
        cost_estimate=SMALL,
    )(weights, *pieces, *waited)


def halves(value, size):
    value = value.reshape(LEVELS, 2, size, WIDE)
    rows = LEVELS * size
    return value[:, 0].reshape(rows, WIDE), value[:, 1].reshape(rows, WIDE)


def join(real_part, imag_part, size):
    shape = (LEVELS, 1, size, WIDE)
    both = jnp.concatenate([real_part.reshape(shape), imag_part.reshape(shape)], axis=1)
    return both.reshape(LEVELS * 2 * size, WIDE)


def close_kernel(parts, size, lane_ref, level_ref, field_ref, *refs):
    rho_refs = refs[:parts]
    out_refs = refs[-parts - 3:-3]
    grad_ref, work_a, work_b = refs[-3:]
    step = pl.program_id(0)

    @pl.when(step == 0)
    def _():
        grad_ref[...] = jnp.zeros_like(grad_ref)

    flat = field_ref.reshape(LEVELS * 2 * size, WIDE)
    real_part, imag_part = lane_apply(lane_ref, 0, *halves(flat[...], size))
    work_a[...] = join(real_part, imag_part, size)

    rho = jnp.concatenate([ref[...] for ref in rho_refs], axis=0)
    rho_real, rho_imag = halves(rho, size)
    real_part, imag_part = lane_apply(lane_ref, 1, rho_real, rho_imag)
    work_b[...] = join(real_part, imag_part, size)

    mid = level_apply(level_ref[0], gather_levels([work_a], size, 0), gather_levels([work_a], size, 1))
    seen = level_apply(level_ref[1], gather_levels([work_b], size, 0), gather_levels([work_b], size, 1))
    terms = seen[:LEVELS] * mid[LEVELS:] - seen[LEVELS:] * mid[:LEVELS]
    total = terms[:, :WIDE]
    for place in range(1, size):
        total = total + terms[:, place * WIDE:(place + 1) * WIDE]
    grad_ref[1] += total

    last = level_apply(level_ref[2], mid[:LEVELS], mid[LEVELS:])
    scatter_levels(work_a, size, 0, last[:LEVELS])
    scatter_levels(work_a, size, 1, last[LEVELS:])
    real_part, imag_part = lane_apply(lane_ref, 2, *halves(work_a[...], size))
    terms = rho_real * imag_part - rho_imag * real_part
    grad_ref[0] += jnp.sum(terms.reshape(LEVELS, size, WIDE), axis=1)
    made = join(real_part, imag_part, size)
    rows = made.shape[0] // parts
    for part in range(parts):
        out_refs[part][...] = made[part * rows:(part + 1) * rows]


def close_columns(field, rho_pieces, lane, level, size, waited):
    total_first, firsts = field.shape[:2]
    devs = total_first // firsts
    parts = len(rho_pieces)
    rows = LEVELS * 2 * size
    field = field.reshape(devs, firsts, firsts * 2 * size, WIDE)
    piece = rho_pieces[0]
    piece_spec = pl.BlockSpec((None,) + piece.shape[1:], lambda i: (i, 0, 0))
    outs = pl.pallas_call(
        functools.partial(close_kernel, parts, size),
        grid=(firsts,),
        in_specs=[
            pl.BlockSpec(lane.shape, lambda i: (0, 0, 0, 0)),
            pl.BlockSpec(level.shape, lambda i: (0, 0, 0)),
            pl.BlockSpec((devs, None, firsts * 2 * size, WIDE), lambda i: (0, i, 0, 0)),
        ]
        + [piece_spec] * parts
        + [pl.BlockSpec(memory_space=pl.ANY)] * len(waited),
        out_specs=[piece_spec] * parts + [pl.BlockSpec((2, LEVELS, WIDE), lambda i: (0, 0, 0))],
        out_shape=[jax.ShapeDtypeStruct(piece.shape, F32)] * parts
        + [jax.ShapeDtypeStruct((2, LEVELS, WIDE), F32)],
        scratch_shapes=[pltpu.VMEM((rows, WIDE), F32), pltpu.VMEM((rows, WIDE), F32)],
        compiler_params=PARAMS,
        cost_estimate=LARGE,
    )(lane, level, field, *rho_pieces, *waited)
    return list(outs[:parts]), outs[parts]


def place_kernel(parts, size, aliased, seat_ref, *refs):
    pieces = refs[:parts]
    out_ref = refs[parts + aliased]
    seat = seat_ref[0]
    levels = pieces[0].shape[0] // (2 * size)
    for step in range(parts):
        part = lax.bitwise_xor(seat, step)
        for half in range(2):
            for level in range(levels):
                start = level * 2 * size + half * size
                out_ref[half, part, :, level * WIDE:(level + 1) * WIDE] = pieces[step][
                    start:start + size, :
                ]


def place_pieces(pieces, seat, held, chunk, shape, size):
    parts = len(pieces)
    firsts, chunks = shape[1], shape[3]
    aliased = 0 if held is None else 1
    piece = pieces[0]
    cols = shape[-1]
    return pl.pallas_call(
        functools.partial(place_kernel, parts, size, aliased),
        grid=(firsts,),
        in_specs=[pl.BlockSpec(memory_space=pltpu.SMEM)]
        + [pl.BlockSpec((None,) + piece.shape[1:], lambda i: (i, 0, 0))] * parts
        + [pl.BlockSpec(memory_space=pl.ANY)] * aliased,
        out_specs=pl.BlockSpec(
            (2, None, parts, None, size, cols), lambda i: (0, i, 0, chunk, 0, 0)
        ),
        out_shape=jax.ShapeDtypeStruct(shape, F32),
        input_output_aliases={parts + 1: 0} if aliased else {},
        compiler_params=PARAMS,
        cost_estimate=SMALL,
    )(seat, *pieces, *([held] if aliased else []))


def swap(pieces, parts):
    moved = [pieces[0]]
    for step in range(1, parts):
        pairs = [(member, member ^ step) for member in range(parts)]
        moved.append(lax.ppermute(pieces[step], "grp", pairs))
    return moved


def grad_kernel(parts, count, seat_ref, *refs):
    out_ref = refs[-1]
    grad = refs[0][...]
    for ref in refs[1:count]:
        grad = grad + ref[...]
    grad = -2.0 * grad
    width = LEVELS // parts
    order = pick_matrix(
        LEVELS, lambda row: lax.bitwise_xor(row // width, seat_ref[0]) * width + row % width
    )
    fold = (grid_of((WIDE, LEVELS), 0) // TRANSMON == grid_of((WIDE, LEVELS), 1)).astype(F32)
    for layer in range(2):
        firsts = exact(jnp.ones((8, WIDE), F32), grad[layer], (((1,), (1,)), ((), ())))
        if layer == 0:
            firsts = exact(firsts, order)
        seconds = exact(exact(jnp.ones((8, LEVELS), F32), grad[layer]), fold)
        out_ref[2 * layer:2 * layer + 1, :] = firsts[:1]
        out_ref[2 * layer + 1:2 * layer + 2, :] = seconds[:1]


def device_grad(grads, seat, parts, waited):
    return pl.pallas_call(
        functools.partial(grad_kernel, parts, len(grads)),
        in_specs=[pl.BlockSpec(memory_space=pltpu.SMEM)]
        + [pl.BlockSpec(memory_space=pltpu.VMEM)] * len(grads)
        + [pl.BlockSpec(memory_space=pl.ANY)] * len(waited),
        out_specs=pl.BlockSpec(memory_space=pltpu.VMEM),
        out_shape=jax.ShapeDtypeStruct((4, LEVELS), F32),
        compiler_params=PARAMS,
        cost_estimate=SMALL,
    )(seat, *grads, *waited)


def grand_total(value):
    rounds = []
    for axis in ("grp", "dev"):
        count = lax.axis_size(axis)
        rounds.append([(axis, 1 << bit, count) for bit in range(count.bit_length() - 1)])
    for axis, step, count in rounds[0][:1] + rounds[1] + rounds[0][1:]:
        pairs = [(member, member ^ step) for member in range(count)]
        value = value + lax.ppermute(value, axis, pairs)
    return value


def per_device(density, costate, phases, displacements, table_slot, checkpoint):
    parts = lax.axis_size("grp")
    share = WIDE // parts
    chunks = max(1, min(4, share // 8))
    size = share // chunks
    seat = lax.axis_index("grp").astype(jnp.int32)
    seats = seat.reshape(1)
    rows, cols = costate.shape[1:]

    opened, turned_by, level, lane = make_weights(
        phases, displacements, table_slot, checkpoint, seats, parts, chunks
    )
    state_cut = open_state(costate, opened, parts, size, 0, 1, [])
    if chunks > 1:
        state_cut += open_state(
            costate, opened, parts, size, 1, chunks - 1, list(state_cut[0][:1])
        )
    rho = [
        cut_pieces(density, seats, parts, chunk, size, list(state_cut[-1][:1]))
        for chunk in range(chunks)
    ]
    state = [swap(pieces, parts) for pieces in state_cut]
    rho_there = [swap(pieces, parts) for pieces in rho]

    shape = (2, rows // WIDE, parts, chunks, size, cols)
    fields, closed, made, grads = [], [], [], []

    def close(chunk):
        waited = closed[chunk - 1][:1] if chunk > 0 else []
        waited = waited + (list(made[chunk - 2][1:]) if chunk > 1 else [])
        out, grad = close_columns(
            fields[chunk], rho_there[chunk], lane, level, size, waited
        )
        closed.append(out)
        made.append(swap(out, parts))
        grads.append(grad)

    for chunk in range(chunks):
        waited = [pieces[0] for pieces in rho] if chunk == 0 else [field]
        if chunk > 1:
            close(chunk - 2)
            waited = waited + closed[chunk - 2][:1]
        field = turn_columns(state[chunk], turned_by, size, waited)
        fields.append(lax.all_to_all(field, "dev", split_axis=0, concat_axis=0, tiled=True))
    for chunk in range(len(made), chunks):
        close(chunk)
    whole = None
    for chunk in range(chunks):
        whole = place_pieces(made[chunk], seats, whole, chunk, shape, size)
    grad = grand_total(device_grad(grads, seats, parts, made[-1][2:3]))
    return whole.reshape(costate.shape), grad.reshape(2, 2, LEVELS)


def solution(mesh):
    return jax.shard_map(
        per_device,
        mesh=mesh,
        in_specs=(P(None, "dev", "grp"), P(None, "dev", "grp"), P(), P(), P(), P()),
        out_specs=(P(None, "dev", "grp"), P()),
        check_vma=False,
    )
```

profile of v0, /device:TPU:0, one launch (start us, length us, event | category | flops | bytes accessed | tf_op | source)
XLA Modules:
  0.0 700.4 jit_solution(8615245028882441820)
XLA Ops:
  1.3 1.9 copy-done.2
  4.6 2.6 shard_map.77
  8.1 16.1 %shard_map.78 = (f32[8,256,128]{2,1,0:T(8,128)S(1)}, f32[8,256,128]{2,1,0:T(8,128)S(1)}, f32[8,256,128]{2,1,0:T(8,128)S(1)}, f32[8,256,128]{2,1,0:T(8,128)S(1)}) custom-call(bf16[2,64,256]{2,1,0:T(8,128)(2,1)S(1)} %slice.7.weight_ref, f32[2,1024,2048]{2,1,0:T(8,128)} %field_ref.3), custom_call_target="tpu_custom_call" | custom-call | flops 1024 | bytes 1024 | tf_op jit(solution)/shard_map/pallas_call | solution.py:189
  25.7 2.5 collective-permute-start.10
  28.3 18.7 %shard_map.79 = (f32[8,256,128]{2,1,0:T(8,128)S(1)}, f32[8,256,128]{2,1,0:T(8,128)S(1)}, f32[8,256,128]{2,1,0:T(8,128)S(1)}, f32[8,256,128]{2,1,0:T(8,128)S(1)},...) custom-call(bf16[2,192,256]{2,1,0:T(8,128)(2,1)S(1)} %slice.6.weight, ...), custom_call_target="tpu_custom_call" | custom-call | flops 1024 | bytes 1024 | tf_op jit(solution)/shard_map/pallas_call | solution.py:189
  52.3 6.4 shard_map.83
  59.6 6.3 shard_map.82
  66.9 6.3 shard_map.81
  74.2 4.7 shard_map.80
  81.0 5.5 shard_map.84.refs_4_
  86.4 6.0 all-to-all-start
  96.8 21.9 %collective-permute-done.1.refs_2_ = f32[8,256,128]{2,1,0:T(8,128)S(1)} collective-permute-done((f32[8,256,128]{2,1,0:T(8,128)}, f32[8,256,128]{2,1,0:T(8,128)S(1)}, u32[]{:S(2)}, u32[]{:S(2)}) %collective-permute-start.1) | collective-permute-done | bytes 1048608 | tf_op jit(solution)/shard_map/ppermute | solution.py:419
  120.1 20.2 %collective-permute-done.2.refs_3_ = f32[8,256,128]{2,1,0:T(8,128)S(1)} collective-permute-done((f32[8,256,128]{2,1,0:T(8,128)}, f32[8,256,128]{2,1,0:T(8,128)S(1)}, u32[]{:S(2)}, u32[]{:S(2)}) %collective-permute-start.2) | collective-permute-done | bytes 1048608 | tf_op jit(solution)/shard_map/ppermute | solution.py:419
  142.8 20.9 %collective-permute-done.7.refs_2_ = f32[8,256,128]{2,1,0:T(8,128)S(1)} collective-permute-done((f32[8,256,128]{2,1,0:T(8,128)}, f32[8,256,128]{2,1,0:T(8,128)S(1)}, u32[]{:S(2)}, u32[]{:S(2)}) %collective-permute-start.7) | collective-permute-done | bytes 1048608 | tf_op jit(solution)/shard_map/ppermute | solution.py:419
  165.2 20.1 %collective-permute-done.8.refs_3_ = f32[8,256,128]{2,1,0:T(8,128)S(1)} collective-permute-done((f32[8,256,128]{2,1,0:T(8,128)}, f32[8,256,128]{2,1,0:T(8,128)S(1)}, u32[]{:S(2)}, u32[]{:S(2)}) %collective-permute-start.8) | collective-permute-done | bytes 1048608 | tf_op jit(solution)/shard_map/ppermute | solution.py:419
  185.3 2.2 collective-permute-start.14
  187.4 5.7 shard_map.85.refs_4_
  193.1 15.5 %collective-permute-done.4.refs_2_ = f32[8,256,128]{2,1,0:T(8,128)S(1)} collective-permute-done((f32[8,256,128]{2,1,0:T(8,128)}, f32[8,256,128]{2,1,0:T(8,128)S(1)}, u32[]{:S(2)}, u32[]{:S(2)}) %collective-permute-start.4) | collective-permute-done | bytes 1048608 | tf_op jit(solution)/shard_map/ppermute | solution.py:419
  209.6 20.6 %collective-permute-done.5.refs_3_ = f32[8,256,128]{2,1,0:T(8,128)S(1)} collective-permute-done((f32[8,256,128]{2,1,0:T(8,128)}, f32[8,256,128]{2,1,0:T(8,128)S(1)}, u32[]{:S(2)}, u32[]{:S(2)}) %collective-permute-start.5) | collective-permute-done | bytes 1048608 | tf_op jit(solution)/shard_map/ppermute | solution.py:419
  232.0 21.6 %collective-permute-done.13.refs_2_ = f32[8,256,128]{2,1,0:T(8,128)S(1)} collective-permute-done((f32[8,256,128]{2,1,0:T(8,128)}, f32[8,256,128]{2,1,0:T(8,128)S(1)}, u32[]{:S(2)}, u32[]{:S(2)}) %collective-permute-start.13) | collective-permute-done | bytes 1048608 | tf_op jit(solution)/shard_map/ppermute | solution.py:419
  255.1 20.0 %collective-permute-done.14.refs_3_ = f32[8,256,128]{2,1,0:T(8,128)S(1)} collective-permute-done((f32[8,256,128]{2,1,0:T(8,128)S(1)}, f32[8,256,128]{2,1,0:T(8,128)S(1)}, u32[]{:S(2)}, u32[]{:S(2)}) %collective-permute-start.14) | collective-permute-done | bytes 1048608 | tf_op jit(solution)/shard_map/ppermute | solution.py:419
  276.1 1.9 collective-permute-start.17
  278.0 5.9 all-to-all-start.1
  284.0 17.6 %shard_map.86 = (f32[8,256,128]{2,1,0:T(8,128)S(1)}, f32[8,256,128]{2,1,0:T(8,128)}, f32[8,256,128]{2,1,0:T(8,128)}, f32[8,256,128]{2,1,0:T(8,128)}, f32[2,64,128]{2,1,0:T(8,128)S(1)}) custom-call(bf16[3,2,256,256]{3,2,1,0:T(8,128)(2,1)S(1)} %copy-done.40, bf16[3,256,256]{2,1,0:T(8,128)(2,1)S(1)} %copy-done.44, f32[8,8,128,128]{3,2,1,0:T(8,128)} %bitcast.2.field_ref, ...), custom_call_target="tpu_custom_call" | custom-call | flops 199999995904 | bytes 1024 | tf_op jit(solution)/shard_map/pallas_call | solution.py:358
  301.6 5.5 shard_map.87.refs_4_
  308.0 69.2 %all-to-all-done.1 = f32[64,8,16,128]{3,2,1,0:T(8,128)} async-done(((f32[64,8,16,128]{3,2,1,0:T(8,128)}), f32[64,8,16,128]{3,2,1,0:T(8,128)}, u32[]{:S(2)}, u32[]{:S(2)}) %all-to-all-start.1) | async-done | bytes 4194336 | tf_op jit(solution)/shard_map/all_to_all | solution.py:510
  377.3 4.6 all-to-all-start.3
  383.8 17.5 %shard_map.88 = (f32[8,256,128]{2,1,0:T(8,128)S(1)}, f32[8,256,128]{2,1,0:T(8,128)}, f32[8,256,128]{2,1,0:T(8,128)}, f32[8,256,128]{2,1,0:T(8,128)}, f32[2,64,128]{2,1,0:T(8,128)S(1)}) custom-call(bf16[3,2,256,256]{3,2,1,0:T(8,128)(2,1)S(1)} %copy-done.40, bf16[3,256,256]{2,1,0:T(8,128)(2,1)S(1)} %copy-done.44, f32[8,8,128,128]{3,2,1,0:T(8,128)} %bitcast.3.field_ref, ...), custom_call_target="tpu_custom_call" | custom-call | flops 199999995904 | bytes 1024 | tf_op jit(solution)/shard_map/pallas_call | solution.py:358
  401.4 5.6 shard_map.89
  408.7 65.6 %all-to-all-done.3 = f32[64,8,16,128]{3,2,1,0:T(8,128)} async-done(((f32[64,8,16,128]{3,2,1,0:T(8,128)}), f32[64,8,16,128]{3,2,1,0:T(8,128)}, u32[]{:S(2)}, u32[]{:S(2)}) %all-to-all-start.3) | async-done | bytes 4194336 | tf_op jit(solution)/shard_map/all_to_all | solution.py:510
  474.4 4.7 all-to-all-start.2
  483.2 16.7 %shard_map.90 = (f32[8,256,128]{2,1,0:T(8,128)S(1)}, f32[8,256,128]{2,1,0:T(8,128)S(1)}, f32[8,256,128]{2,1,0:T(8,128)S(1)}, f32[8,256,128]{2,1,0:T(8,128)S(1)}, f32[2,64,128]{2,1,0:T(8,128)S(1)}) custom-call(bf16[3,2,256,256]{3,2,1,0:T(8,128)(2,1)S(1)} %copy-done.41, bf16[3,256,256]{2,1,0:T(8,128)(2,1)S(1)} %copy-done.45, ...), custom_call_target="tpu_custom_call" | custom-call | flops 199999995904 | bytes 1024 | tf_op jit(solution)/shard_map/pallas_call | solution.py:358
  500.9 4.7 collective-permute-done.28.refs_6_.refs_2_
  505.6 21.5 %collective-permute-done.29.refs_7_.refs_3_ = f32[8,256,128]{2,1,0:T(8,128)} collective-permute-done((f32[8,256,128]{2,1,0:T(8,128)}, f32[8,256,128]{2,1,0:T(8,128)}, u32[]{:S(2)}, u32[]{:S(2)}) %collective-permute-start.29) | collective-permute-done | bytes 1048608 | tf_op jit(solution)/shard_map/ppermute | solution.py:419
  527.1 44.5 %all-to-all-done.2 = f32[64,8,16,128]{3,2,1,0:T(8,128)} async-done(((f32[64,8,16,128]{3,2,1,0:T(8,128)}), f32[64,8,16,128]{3,2,1,0:T(8,128)}, u32[]{:S(2)}, u32[]{:S(2)}) %all-to-all-start.2) | async-done | bytes 4194336 | tf_op jit(solution)/shard_map/all_to_all | solution.py:510
  573.7 17.4 %shard_map.91 = (f32[8,256,128]{2,1,0:T(8,128)S(1)}, f32[8,256,128]{2,1,0:T(8,128)}, f32[8,256,128]{2,1,0:T(8,128)S(1)}, f32[8,256,128]{2,1,0:T(8,128)}, f32[2,64,128]{2,1,0:T(8,128)S(1)}) custom-call(bf16[3,2,256,256]{3,2,1,0:T(8,128)(2,1)S(1)} %copy-done.42, bf16[3,256,256]{2,1,0:T(8,128)(2,1)S(1)} %copy-done.46, f32[8,8,128,128]{3,2,1,0:T(8,128)} %bitcast.4.field_ref, ...), custom_call_target="tpu_custom_call" | custom-call | flops 199999995904 | bytes 1024 | tf_op jit(solution)/shard_map/pallas_call | solution.py:358
  591.8 22.4 %collective-permute-done.31.refs_2_.refs_4_ = f32[8,256,128]{2,1,0:T(8,128)S(1)} collective-permute-done((f32[8,256,128]{2,1,0:T(8,128)S(1)}, f32[8,256,128]{2,1,0:T(8,128)S(1)}, u32[]{:S(2)}, u32[]{:S(2)}) %collective-permute-start.31) | collective-permute-done | bytes 1048608 | tf_op jit(solution)/shard_map/ppermute | solution.py:419
  616.3 2.4 collective-permute-start.37
  618.6 1.6 collective-permute-done.37
  621.2 2.6 collective-permute-done.38
  623.8 2.4 collective-permute-start.39
  630.3 6.5 shard_map.92.refs_4_
  636.7 6.6 shard_map.93.refs_4_
  643.3 8.9 %collective-permute-done.34.refs_2_ = f32[8,256,128]{2,1,0:T(8,128)S(1)} collective-permute-done((f32[8,256,128]{2,1,0:T(8,128)S(1)}, f32[8,256,128]{2,1,0:T(8,128)S(1)}, u32[]{:S(2)}, u32[]{:S(2)}) %collective-permute-start.34) | collective-permute-done | bytes 1048608 | tf_op jit(solution)/shard_map/ppermute | solution.py:419
  652.1 21.7 %collective-permute-done.35.refs_3_ = f32[8,256,128]{2,1,0:T(8,128)S(1)} collective-permute-done((f32[8,256,128]{2,1,0:T(8,128)S(1)}, f32[8,256,128]{2,1,0:T(8,128)S(1)}, u32[]{:S(2)}, u32[]{:S(2)}) %collective-permute-start.35) | collective-permute-done | bytes 1048608 | tf_op jit(solution)/shard_map/ppermute | solution.py:419
  673.8 3.5 shard_map.94.refs_4_
  677.3 19.0 %collective-permute-done.32.refs_3_ = f32[8,256,128]{2,1,0:T(8,128)S(1)} collective-permute-done((f32[8,256,128]{2,1,0:T(8,128)}, f32[8,256,128]{2,1,0:T(8,128)S(1)}, u32[]{:S(2)}, u32[]{:S(2)}) %collective-permute-start.32) | collective-permute-done | bytes 1048608 | tf_op jit(solution)/shard_map/ppermute | solution.py:419
  696.3 3.5 shard_map.95
  (169 shorter events, 49.2 us)
Async XLA Ops:
  8.1 179.3 %copy-start.9 = (bf16[256,256]{1,0:T(8,128)(2,1)}, bf16[256,256]{1,0:T(8,128)(2,1)S(1)}, u32[]{:S(2)}) copy-start(bf16[256,256]{1,0:T(8,128)(2,1)S(1)} %get-tuple-element.60.weight_ref) | copy-start | bytes 393220
  25.2 55.7 %collective-permute-start.9 = (f32[8,256,128]{2,1,0:T(8,128)S(1)}, f32[8,256,128]{2,1,0:T(8,128)S(1)}, u32[]{:S(2)}, u32[]{:S(2)}) collective-permute-start(f32[8,256,128]{2,1,0:T(8,128)S(1)} %get-tuple-element.75), channel_id=1, source_target_pairs={{0,8},{8,0},{16,24},{24,16},{1,9},{9,1},{17,25},{25,17},{2,10},{10... | collective-permute-start | bytes 3145736 | tf_op jit(solution)/shard_map/ppermute | solution.py:419
  25.7 55.3 %collective-permute-start.10 = (f32[8,256,128]{2,1,0:T(8,128)S(1)}, f32[8,256,128]{2,1,0:T(8,128)S(1)}, u32[]{:S(2)}, u32[]{:S(2)}) collective-permute-start(f32[8,256,128]{2,1,0:T(8,128)S(1)} %get-tuple-element.76), channel_id=1, source_target_pairs={{0,16},{8,24},{16,0},{24,8},{1,17},{9,25},{17,1},{25,9},{2,18},{10... | collective-permute-start | bytes 3145736 | tf_op jit(solution)/shard_map/ppermute | solution.py:419
  28.2 52.8 %collective-permute-start.11 = (f32[8,256,128]{2,1,0:T(8,128)S(1)}, f32[8,256,128]{2,1,0:T(8,128)S(1)}, u32[]{:S(2)}, u32[]{:S(2)}) collective-permute-start(f32[8,256,128]{2,1,0:T(8,128)S(1)} %get-tuple-element.77), channel_id=1, source_target_pairs={{0,24},{8,16},{16,8},{24,0},{1,25},{9,17},{17,9},{25,1},{2,26},{10... | collective-permute-start | bytes 3145736 | tf_op jit(solution)/shard_map/ppermute | solution.py:419
  86.4 191.5 %all-to-all-start = ((f32[64,8,16,128]{3,2,1,0:T(8,128)}), f32[64,8,16,128]{3,2,1,0:T(8,128)}, u32[]{:S(2)}, u32[]{:S(2)}) async-start(f32[64,8,16,128]{3,2,1,0:T(8,128)} %shard_map.84.refs_4_), calls=%async_computation | async-start | bytes 8388608 | tf_op jit(solution)/shard_map/all_to_all | solution.py:510
  92.5 2.9 collective-permute-start
  92.5 26.2 %collective-permute-start.1 = (f32[8,256,128]{2,1,0:T(8,128)}, f32[8,256,128]{2,1,0:T(8,128)S(1)}, u32[]{:S(2)}, u32[]{:S(2)}) collective-permute-start(f32[8,256,128]{2,1,0:T(8,128)} %get-tuple-element.65), channel_id=1, source_target_pairs={{0,16},{8,24},{16,0},{24,8},{1,17},{9,25},{17,1},{25,9},{2,18},{10... | collective-permute-start | bytes 3145736 | tf_op jit(solution)/shard_map/ppermute | solution.py:419
  94.0 46.3 %collective-permute-start.2 = (f32[8,256,128]{2,1,0:T(8,128)}, f32[8,256,128]{2,1,0:T(8,128)S(1)}, u32[]{:S(2)}, u32[]{:S(2)}) collective-permute-start(f32[8,256,128]{2,1,0:T(8,128)} %get-tuple-element.66), channel_id=1, source_target_pairs={{0,24},{8,16},{16,8},{24,0},{1,25},{9,17},{17,9},{25,1},{2,26},{10... | collective-permute-start | bytes 3145736 | tf_op jit(solution)/shard_map/ppermute | solution.py:419
  94.3 47.4 %collective-permute-start.3 = (f32[8,256,128]{2,1,0:T(8,128)}, f32[8,256,128]{2,1,0:T(8,128)S(1)}, u32[]{:S(2)}, u32[]{:S(2)}) collective-permute-start(f32[8,256,128]{2,1,0:T(8,128)} %get-tuple-element.68), channel_id=1, source_target_pairs={{0,8},{8,0},{16,24},{24,16},{1,9},{9,1},{17,25},{25,17},{2,10},{10... | collective-permute-start | bytes 3145736 | tf_op jit(solution)/shard_map/ppermute | solution.py:419
  94.7 48.1 %collective-permute-start.6 = (f32[8,256,128]{2,1,0:T(8,128)}, f32[8,256,128]{2,1,0:T(8,128)S(1)}, u32[]{:S(2)}, u32[]{:S(2)}) collective-permute-start(f32[8,256,128]{2,1,0:T(8,128)} %copy-done.38), channel_id=1, source_target_pairs={{0,8},{8,0},{16,24},{24,16},{1,9},{9,1},{17,25},{25,17},{2,10},{10... | collective-permute-start | bytes 3145736 | tf_op jit(solution)/shard_map/ppermute | solution.py:419
  95.4 97.8 %copy-start.18 = (f32[8,256,128]{2,1,0:T(8,128)}, f32[8,256,128]{2,1,0:T(8,128)S(1)}, u32[]{:S(2)}) copy-start(f32[8,256,128]{2,1,0:T(8,128)S(1)} %collective-permute-done.refs_1_) | copy-start | bytes 3145732
  95.4 68.3 %collective-permute-start.7 = (f32[8,256,128]{2,1,0:T(8,128)}, f32[8,256,128]{2,1,0:T(8,128)S(1)}, u32[]{:S(2)}, u32[]{:S(2)}) collective-permute-start(f32[8,256,128]{2,1,0:T(8,128)} %copy-done.37), channel_id=1, source_target_pairs={{0,16},{8,24},{16,0},{24,8},{1,17},{9,25},{17,1},{25,9},{2,18},{10... | collective-permute-start | bytes 3145736 | tf_op jit(solution)/shard_map/ppermute | solution.py:419
  119.7 65.5 %collective-permute-start.8 = (f32[8,256,128]{2,1,0:T(8,128)}, f32[8,256,128]{2,1,0:T(8,128)S(1)}, u32[]{:S(2)}, u32[]{:S(2)}) collective-permute-start(f32[8,256,128]{2,1,0:T(8,128)} %copy-done.36), channel_id=1, source_target_pairs={{0,24},{8,16},{16,8},{24,0},{1,25},{9,17},{17,9},{25,1},{2,26},{10... | collective-permute-start | bytes 3145736 | tf_op jit(solution)/shard_map/ppermute | solution.py:419
  140.3 68.3 %collective-permute-start.4 = (f32[8,256,128]{2,1,0:T(8,128)}, f32[8,256,128]{2,1,0:T(8,128)S(1)}, u32[]{:S(2)}, u32[]{:S(2)}) collective-permute-start(f32[8,256,128]{2,1,0:T(8,128)} %get-tuple-element.69), channel_id=1, source_target_pairs={{0,16},{8,24},{16,0},{24,8},{1,17},{9,25},{17,1},{25,9},{2,18},{10... | collective-permute-start | bytes 3145736 | tf_op jit(solution)/shard_map/ppermute | solution.py:419
  141.8 88.4 %collective-permute-start.5 = (f32[8,256,128]{2,1,0:T(8,128)}, f32[8,256,128]{2,1,0:T(8,128)S(1)}, u32[]{:S(2)}, u32[]{:S(2)}) collective-permute-start(f32[8,256,128]{2,1,0:T(8,128)} %get-tuple-element.70), channel_id=1, source_target_pairs={{0,24},{8,16},{16,8},{24,0},{1,25},{9,17},{17,9},{25,1},{2,26},{10... | collective-permute-start | bytes 3145736 | tf_op jit(solution)/shard_map/ppermute | solution.py:419
  142.8 89.1 %collective-permute-start.12 = (f32[8,256,128]{2,1,0:T(8,128)}, f32[8,256,128]{2,1,0:T(8,128)S(1)}, u32[]{:S(2)}, u32[]{:S(2)}) collective-permute-start(f32[8,256,128]{2,1,0:T(8,128)} %copy-done.35), channel_id=1, source_target_pairs={{0,8},{8,0},{16,24},{24,16},{1,9},{9,1},{17,25},{25,17},{2,10},{10... | collective-permute-start | bytes 3145736 | tf_op jit(solution)/shard_map/ppermute | solution.py:419
  163.7 89.9 %collective-permute-start.13 = (f32[8,256,128]{2,1,0:T(8,128)}, f32[8,256,128]{2,1,0:T(8,128)S(1)}, u32[]{:S(2)}, u32[]{:S(2)}) collective-permute-start(f32[8,256,128]{2,1,0:T(8,128)} %copy-done.34), channel_id=1, source_target_pairs={{0,16},{8,24},{16,0},{24,8},{1,17},{9,25},{17,1},{25,9},{2,18},{10... | collective-permute-start | bytes 3145736 | tf_op jit(solution)/shard_map/ppermute | solution.py:419
  185.3 89.8 %collective-permute-start.14 = (f32[8,256,128]{2,1,0:T(8,128)S(1)}, f32[8,256,128]{2,1,0:T(8,128)S(1)}, u32[]{:S(2)}, u32[]{:S(2)}) collective-permute-start(f32[8,256,128]{2,1,0:T(8,128)S(1)} %get-tuple-element.84), channel_id=1, source_target_pairs={{0,24},{8,16},{16,8},{24,0},{1,25},{9,17},{17,9},{25,1},{2,26},{10... | collective-permute-start | bytes 3145736 | tf_op jit(solution)/shard_map/ppermute | solution.py:419
  209.6 97.5 %collective-permute-start.18 = (f32[8,256,128]{2,1,0:T(8,128)}, f32[8,256,128]{2,1,0:T(8,128)}, u32[]{:S(2)}, u32[]{:S(2)}) collective-permute-start(f32[8,256,128]{2,1,0:T(8,128)} %get-tuple-element.90), channel_id=1, source_target_pairs={{0,8},{8,0},{16,24},{24,16},{1,9},{9,1},{17,25},{25,17},{2,10},{10... | collective-permute-start | bytes 3145736 | tf_op jit(solution)/shard_map/ppermute | solution.py:419
  231.2 76.4 %collective-permute-start.21 = (f32[8,256,128]{2,1,0:T(8,128)}, f32[8,256,128]{2,1,0:T(8,128)}, u32[]{:S(2)}, u32[]{:S(2)}) collective-permute-start(f32[8,256,128]{2,1,0:T(8,128)} %get-tuple-element.93), channel_id=1, source_target_pairs={{0,8},{8,0},{16,24},{24,16},{1,9},{9,1},{17,25},{25,17},{2,10},{10... | collective-permute-start | bytes 3145736 | tf_op jit(solution)/shard_map/ppermute | solution.py:419
  231.9 149.9 %collective-permute-start.15 = (f32[8,256,128]{2,1,0:T(8,128)}, f32[8,256,128]{2,1,0:T(8,128)}, u32[]{:S(2)}, u32[]{:S(2)}) collective-permute-start(f32[8,256,128]{2,1,0:T(8,128)} %get-tuple-element.86), channel_id=1, source_target_pairs={{0,8},{8,0},{16,24},{24,16},{1,9},{9,1},{17,25},{25,17},{2,10},{10... | collective-permute-start | bytes 3145736 | tf_op jit(solution)/shard_map/ppermute | solution.py:419
  253.6 128.4 %collective-permute-start.16 = (f32[8,256,128]{2,1,0:T(8,128)}, f32[8,256,128]{2,1,0:T(8,128)}, u32[]{:S(2)}, u32[]{:S(2)}) collective-permute-start(f32[8,256,128]{2,1,0:T(8,128)} %get-tuple-element.87), channel_id=1, source_target_pairs={{0,16},{8,24},{16,0},{24,8},{1,17},{9,25},{17,1},{25,9},{2,18},{10... | collective-permute-start | bytes 3145736 | tf_op jit(solution)/shard_map/ppermute | solution.py:419
  276.1 106.5 %collective-permute-start.17 = (f32[8,256,128]{2,1,0:T(8,128)}, f32[8,256,128]{2,1,0:T(8,128)}, u32[]{:S(2)}, u32[]{:S(2)}) collective-permute-start(f32[8,256,128]{2,1,0:T(8,128)} %get-tuple-element.88), channel_id=1, source_target_pairs={{0,24},{8,16},{16,8},{24,0},{1,25},{9,17},{17,9},{25,1},{2,26},{10... | collective-permute-start | bytes 3145736 | tf_op jit(solution)/shard_map/ppermute | solution.py:419
  278.0 99.3 %all-to-all-start.1 = ((f32[64,8,16,128]{3,2,1,0:T(8,128)}), f32[64,8,16,128]{3,2,1,0:T(8,128)}, u32[]{:S(2)}, u32[]{:S(2)}) async-start(f32[64,8,16,128]{3,2,1,0:T(8,128)} %shard_map.85.refs_4_), calls=%async_computation.1 | async-start | bytes 8388608 | tf_op jit(solution)/shard_map/all_to_all | solution.py:510
  307.1 100.0 %collective-permute-start.22 = (f32[8,256,128]{2,1,0:T(8,128)}, f32[8,256,128]{2,1,0:T(8,128)}, u32[]{:S(2)}, u32[]{:S(2)}) collective-permute-start(f32[8,256,128]{2,1,0:T(8,128)} %get-tuple-element.94), channel_id=1, source_target_pairs={{0,16},{8,24},{16,0},{24,8},{1,17},{9,25},{17,1},{25,9},{2,18},{10... | collective-permute-start | bytes 3145736 | tf_op jit(solution)/shard_map/ppermute | solution.py:419
  307.6 100.1 %collective-permute-start.23 = (f32[8,256,128]{2,1,0:T(8,128)}, f32[8,256,128]{2,1,0:T(8,128)}, u32[]{:S(2)}, u32[]{:S(2)}) collective-permute-start(f32[8,256,128]{2,1,0:T(8,128)} %get-tuple-element.95), channel_id=1, source_target_pairs={{0,24},{8,16},{16,8},{24,0},{1,25},{9,17},{17,9},{25,1},{2,26},{10... | collective-permute-start | bytes 3145736 | tf_op jit(solution)/shard_map/ppermute | solution.py:419
  377.3 97.1 %all-to-all-start.3 = ((f32[64,8,16,128]{3,2,1,0:T(8,128)}), f32[64,8,16,128]{3,2,1,0:T(8,128)}, u32[]{:S(2)}, u32[]{:S(2)}) async-start(f32[64,8,16,128]{3,2,1,0:T(8,128)} %shard_map.87.refs_4_), calls=%async_computation.3 | async-start | bytes 8388608 | tf_op jit(solution)/shard_map/all_to_all | solution.py:510
  381.8 97.3 %collective-permute-start.24 = (f32[8,256,128]{2,1,0:T(8,128)}, f32[8,256,128]{2,1,0:T(8,128)}, u32[]{:S(2)}, u32[]{:S(2)}) collective-permute-start(f32[8,256,128]{2,1,0:T(8,128)} %get-tuple-element.96), channel_id=1, source_target_pairs={{0,8},{8,0},{16,24},{24,16},{1,9},{9,1},{17,25},{25,17},{2,10},{10... | collective-permute-start | bytes 3145736 | tf_op jit(solution)/shard_map/ppermute | solution.py:419
  381.9 97.3 %collective-permute-start.25 = (f32[8,256,128]{2,1,0:T(8,128)}, f32[8,256,128]{2,1,0:T(8,128)}, u32[]{:S(2)}, u32[]{:S(2)}) collective-permute-start(f32[8,256,128]{2,1,0:T(8,128)} %get-tuple-element.97), channel_id=1, source_target_pairs={{0,16},{8,24},{16,0},{24,8},{1,17},{9,25},{17,1},{25,9},{2,18},{10... | collective-permute-start | bytes 3145736 | tf_op jit(solution)/shard_map/ppermute | solution.py:419
  382.7 97.3 %collective-permute-start.26 = (f32[8,256,128]{2,1,0:T(8,128)}, f32[8,256,128]{2,1,0:T(8,128)}, u32[]{:S(2)}, u32[]{:S(2)}) collective-permute-start(f32[8,256,128]{2,1,0:T(8,128)} %get-tuple-element.98), channel_id=1, source_target_pairs={{0,24},{8,16},{16,8},{24,0},{1,25},{9,17},{17,9},{25,1},{2,26},{10... | collective-permute-start | bytes 3145736 | tf_op jit(solution)/shard_map/ppermute | solution.py:419
  407.0 93.9 %collective-permute-start.19 = (f32[8,256,128]{2,1,0:T(8,128)}, f32[8,256,128]{2,1,0:T(8,128)}, u32[]{:S(2)}, u32[]{:S(2)}) collective-permute-start(f32[8,256,128]{2,1,0:T(8,128)} %get-tuple-element.91), channel_id=1, source_target_pairs={{0,16},{8,24},{16,0},{24,8},{1,17},{9,25},{17,1},{25,9},{2,18},{10... | collective-permute-start | bytes 3145736 | tf_op jit(solution)/shard_map/ppermute | solution.py:419
  407.7 93.2 %collective-permute-start.20 = (f32[8,256,128]{2,1,0:T(8,128)}, f32[8,256,128]{2,1,0:T(8,128)}, u32[]{:S(2)}, u32[]{:S(2)}) collective-permute-start(f32[8,256,128]{2,1,0:T(8,128)} %get-tuple-element.92), channel_id=1, source_target_pairs={{0,24},{8,16},{16,8},{24,0},{1,25},{9,17},{17,9},{25,1},{2,26},{10... | collective-permute-start | bytes 3145736 | tf_op jit(solution)/shard_map/ppermute | solution.py:419
  474.4 97.2 %all-to-all-start.2 = ((f32[64,8,16,128]{3,2,1,0:T(8,128)}), f32[64,8,16,128]{3,2,1,0:T(8,128)}, u32[]{:S(2)}, u32[]{:S(2)}) async-start(f32[64,8,16,128]{3,2,1,0:T(8,128)} %shard_map.89), calls=%async_computation.2 | async-start | bytes 8388608 | tf_op jit(solution)/shard_map/all_to_all | solution.py:510
  479.1 21.8 %collective-permute-start.27 = (f32[8,256,128]{2,1,0:T(8,128)}, f32[8,256,128]{2,1,0:T(8,128)}, u32[]{:S(2)}, u32[]{:S(2)}) collective-permute-start(f32[8,256,128]{2,1,0:T(8,128)} %get-tuple-element.100), channel_id=1, source_target_pairs={{0,8},{8,0},{16,24},{24,16},{1,9},{9,1},{17,25},{25,17},{2,10},{10... | collective-permute-start | bytes 3145736 | tf_op jit(solution)/shard_map/ppermute | solution.py:419
  479.2 26.3 %collective-permute-start.28 = (f32[8,256,128]{2,1,0:T(8,128)}, f32[8,256,128]{2,1,0:T(8,128)}, u32[]{:S(2)}, u32[]{:S(2)}) collective-permute-start(f32[8,256,128]{2,1,0:T(8,128)} %get-tuple-element.101), channel_id=1, source_target_pairs={{0,16},{8,24},{16,0},{24,8},{1,17},{9,25},{17,1},{25,9},{2,18},{10... | collective-permute-start | bytes 3145736 | tf_op jit(solution)/shard_map/ppermute | solution.py:419
  479.9 47.1 %collective-permute-start.29 = (f32[8,256,128]{2,1,0:T(8,128)}, f32[8,256,128]{2,1,0:T(8,128)}, u32[]{:S(2)}, u32[]{:S(2)}) collective-permute-start(f32[8,256,128]{2,1,0:T(8,128)} %get-tuple-element.102), channel_id=1, source_target_pairs={{0,24},{8,16},{16,8},{24,0},{1,25},{9,17},{17,9},{25,1},{2,26},{10... | collective-permute-start | bytes 3145736 | tf_op jit(solution)/shard_map/ppermute | solution.py:419
  573.7 56.6 %copy-start.6 = (f32[8,256,128]{2,1,0:T(8,128)S(1)}, f32[8,256,128]{2,1,0:T(8,128)}, u32[]{:S(2)}) copy-start(f32[8,256,128]{2,1,0:T(8,128)} %copy-done.5) | copy-start | bytes 3145732
  591.1 23.1 %collective-permute-start.31 = (f32[8,256,128]{2,1,0:T(8,128)S(1)}, f32[8,256,128]{2,1,0:T(8,128)S(1)}, u32[]{:S(2)}, u32[]{:S(2)}) collective-permute-start(f32[8,256,128]{2,1,0:T(8,128)S(1)} %get-tuple-element.105), channel_id=1, source_target_pairs={{0,16},{8,24},{16,0},{24,8},{1,17},{9,25},{17,1},{25,9},{2,18},{10... | collective-permute-start | bytes 3145736 | tf_op jit(solution)/shard_map/ppermute | solution.py:419
  615.1 1.2 collective-permute-start.36
  616.3 3.9 collective-permute-start.37
  620.2 3.6 collective-permute-start.38
  623.8 4.5 collective-permute-start.39
  626.2 2.7 collective-permute-start.33
  626.2 26.0 %collective-permute-start.34 = (f32[8,256,128]{2,1,0:T(8,128)S(1)}, f32[8,256,128]{2,1,0:T(8,128)S(1)}, u32[]{:S(2)}, u32[]{:S(2)}) collective-permute-start(f32[8,256,128]{2,1,0:T(8,128)S(1)} %get-tuple-element.108), channel_id=1, source_target_pairs={{0,16},{8,24},{16,0},{24,8},{1,17},{9,25},{17,1},{25,9},{2,18},{10... | collective-permute-start | bytes 3145736 | tf_op jit(solution)/shard_map/ppermute | solution.py:419
  626.9 47.0 %collective-permute-start.35 = (f32[8,256,128]{2,1,0:T(8,128)S(1)}, f32[8,256,128]{2,1,0:T(8,128)S(1)}, u32[]{:S(2)}, u32[]{:S(2)}) collective-permute-start(f32[8,256,128]{2,1,0:T(8,128)S(1)} %get-tuple-element.109), channel_id=1, source_target_pairs={{0,24},{8,16},{16,8},{24,0},{1,25},{9,17},{17,9},{25,1},{2,26},{10... | collective-permute-start | bytes 3145736 | tf_op jit(solution)/shard_map/ppermute | solution.py:419
  628.0 49.3 %collective-permute-start.30 = (f32[8,256,128]{2,1,0:T(8,128)}, f32[8,256,128]{2,1,0:T(8,128)S(1)}, u32[]{:S(2)}, u32[]{:S(2)}) collective-permute-start(f32[8,256,128]{2,1,0:T(8,128)} %get-tuple-element.104), channel_id=1, source_target_pairs={{0,8},{8,0},{16,24},{24,16},{1,9},{9,1},{17,25},{25,17},{2,10},{10... | collective-permute-start | bytes 3145736 | tf_op jit(solution)/shard_map/ppermute | solution.py:419
  628.3 68.0 %collective-permute-start.32 = (f32[8,256,128]{2,1,0:T(8,128)}, f32[8,256,128]{2,1,0:T(8,128)S(1)}, u32[]{:S(2)}, u32[]{:S(2)}) collective-permute-start(f32[8,256,128]{2,1,0:T(8,128)} %get-tuple-element.106), channel_id=1, source_target_pairs={{0,24},{8,16},{16,8},{24,0},{1,25},{9,17},{17,9},{25,1},{2,26},{10... | collective-permute-start | bytes 3145736 | tf_op jit(solution)/shard_map/ppermute | solution.py:419
  628.9 70.9 %collective-permute-start.40 = (f32[4,64]{1,0:T(4,128)S(1)}, f32[4,64]{1,0:T(4,128)S(1)}, u32[]{:S(2)}, u32[]{:S(2)}) collective-permute-start(f32[4,64]{1,0:T(4,128)S(1)} %add.18), channel_id=1, source_target_pairs={{0,16},{8,24},{16,0},{24,8},{1,17},{9,25},{17,1},{25,9},{2,18},{10... | collective-permute-start | bytes 3080 | tf_op jit(solution)/shard_map/ppermute | solution.py:463
  (47 other events, 469.7 us)
where the time goes:
time: 703 us; the launch traced here: 700 us
  waiting for transfers between devices  444 us (63%)
  Pallas kernels  174 us (25%)
  starting transfers between devices  55.9 us (8%)
  local copies, waits for them, and re-layouts  24.5 us (3%)
    ppermute x36, waiting for transfers between devices, swap(): moved.append(lax.ppermute(pieces[step], 'grp', pairs))  260 us
    all_to_all x4, waiting for transfers between devices, per_device(): lax.all_to_all(field, 'dev', split_axis=0, concat_axis=0, tiled=True)  179 us
    pallas_call x4, Pallas kernels, close_columns(): pl.pallas_call(functools.partial(close_kernel, parts, size), grid=(firsts...  69.2 us
    pallas_call x2, Pallas kernels, open_state(): pl.pallas_call(functools.partial(open_kernel, count, len(waited)), grid=(...  34.9 us
    ppermute x36, starting transfers between devices, swap(): moved.append(lax.ppermute(pieces[step], 'grp', pairs))  27.4 us
    unnamed x100, local copies, waits for them, and re-layouts  24.5 us
    pallas_call x4, Pallas kernels, cut_pieces(): pl.pallas_call(functools.partial(cut_kernel, size, len(waited)), grid=(fi...  23.7 us
    pallas_call x4, Pallas kernels, turn_columns(): pl.pallas_call(functools.partial(turn_kernel, parts, size), grid=(firsts,...  22.2 us
  transfers between devices with their start and end apart: 45, of which 21 were waited for; matrix products, arithmetic and copies ran while one was open for 0% of the time, Pallas kernels for 19%

commit v1 on v0

--- a/solution.py
+++ b/solution.py
@@ -485,7 +485,7 @@
         cut_pieces(density, seats, parts, chunk, size, list(state_cut[-1][:1]))
         for chunk in range(chunks)
     ]
-    state = [swap(pieces, parts) for pieces in state_cut]
+    state = [swap(pieces, parts) for pieces in state_cut[:2]]
     rho_there = [swap(pieces, parts) for pieces in rho]
 
     shape = (2, rows // WIDE, parts, chunks, size, cols)
@@ -493,7 +493,10 @@
 
     def close(chunk):
         waited = closed[chunk - 1][:1] if chunk > 0 else []
-        waited = waited + (list(made[chunk - 2][1:]) if chunk > 1 else [])
+        if chunk == chunks - 1 and chunk > 0:
+            waited = waited + list(made[chunk - 1][1:])
+        elif chunk > 1:
+            waited = waited + list(made[chunk - 2][1:])
         out, grad = close_columns(
             fields[chunk], rho_there[chunk], lane, level, size, waited
         )
@@ -508,12 +511,15 @@
             waited = waited + closed[chunk - 2][:1]
         field = turn_columns(state[chunk], turned_by, size, waited)
         fields.append(lax.all_to_all(field, "dev", split_axis=0, concat_axis=0, tiled=True))
+        if chunk + 2 < chunks:
+            pieces, fields[chunk] = lax.optimization_barrier((state_cut[chunk + 2], fields[chunk]))
+            state.append(swap(pieces, parts))
     for chunk in range(len(made), chunks):
         close(chunk)
     whole = None
     for chunk in range(chunks):
         whole = place_pieces(made[chunk], seats, whole, chunk, shape, size)
-    grad = grand_total(device_grad(grads, seats, parts, made[-1][2:3]))
+    grad = grand_total(device_grad(grads, seats, parts, made[-1][1:]))
     return whole.reshape(costate.shape), grad.reshape(2, 2, LEVELS)
 
 

time: 703 us -> 680 us (0.967)
  waiting for transfers between devices: 444 us -> 420 us
    all_to_all x4, waiting for transfers between devices: 179 us -> 136 us  [per_device(): lax.all_to_all(field, 'dev', split_axis=0, concat_axis=0, tiled=True)]
    ppermute x36, waiting for transfers between devices: 260 us -> 277 us  [swap(): moved.append(lax.ppermute(pieces[step], 'grp', pairs))]
    unnamed x100 -> x88, local copies, waits for them, and re-layouts: 24.5 us -> 22.3 us
  transfers between devices with their start and end apart: 45 -> 45, of which waited for: 21 -> 26; matrix products, arithmetic and copies ran while one was open for 0% -> 0% of each run, Pallas kernels for 19% -> 20%
where the time goes in v1:
time: 680 us; the launch traced here: 678 us
  waiting for transfers between devices  420 us (62%)
  Pallas kernels  174 us (26%)
  starting transfers between devices  59.1 us (9%)
  local copies, waits for them, and re-layouts  22.3 us (3%)
    ppermute x36, waiting for transfers between devices, swap(): moved.append(lax.ppermute(pieces[step], 'grp', pairs))  277 us
    all_to_all x4, waiting for transfers between devices, per_device(): lax.all_to_all(field, 'dev', split_axis=0, concat_axis=0, tiled=True)  136 us
    pallas_call x4, Pallas kernels, close_columns(): pl.pallas_call(functools.partial(close_kernel, parts, size), grid=(firsts...  69.2 us
    pallas_call x2, Pallas kernels, open_state(): pl.pallas_call(functools.partial(open_kernel, count, len(waited)), grid=(...  35 us
    ppermute x36, starting transfers between devices, swap(): moved.append(lax.ppermute(pieces[step], 'grp', pairs))  30.5 us
    pallas_call x4, Pallas kernels, turn_columns(): pl.pallas_call(functools.partial(turn_kernel, parts, size), grid=(firsts,...  25.1 us
    pallas_call x4, Pallas kernels, cut_pieces(): pl.pallas_call(functools.partial(cut_kernel, size, len(waited)), grid=(fi...  24.7 us
    unnamed x88, local copies, waits for them, and re-layouts  22.3 us
  transfers between devices with their start and end apart: 45, of which 26 were waited for; matrix products, arithmetic and copies ran while one was open for 0% of the time, Pallas kernels for 20%

profile of v1, /device:TPU:0, one launch (start us, length us, event | category | flops | bytes accessed | tf_op | source)
XLA Modules:
  0.0 677.7 jit_solution(9316575946930523858)
XLA Ops:
  4.6 2.6 shard_map.77
  8.0 16.3 %shard_map.78 = (f32[8,256,128]{2,1,0:T(8,128)S(1)}, f32[8,256,128]{2,1,0:T(8,128)S(1)}, f32[8,256,128]{2,1,0:T(8,128)S(1)}, f32[8,256,128]{2,1,0:T(8,128)S(1)}) custom-call(bf16[2,64,256]{2,1,0:T(8,128)(2,1)S(1)} %slice.7.weight_ref, f32[2,1024,2048]{2,1,0:T(8,128)} %field_ref.3), custom_call_target="tpu_custom_call" | custom-call | flops 1024 | bytes 1024 | tf_op jit(solution)/shard_map/pallas_call | solution.py:189
  25.7 2.5 collective-permute-start.4
  28.3 18.7 %shard_map.79 = (f32[8,256,128]{2,1,0:T(8,128)S(1)}, f32[8,256,128]{2,1,0:T(8,128)S(1)}, f32[8,256,128]{2,1,0:T(8,128)S(1)}, f32[8,256,128]{2,1,0:T(8,128)S(1)},...) custom-call(bf16[2,192,256]{2,1,0:T(8,128)(2,1)S(1)} %slice.6.weight, ...), custom_call_target="tpu_custom_call" | custom-call | flops 1024 | bytes 1024 | tf_op jit(solution)/shard_map/pallas_call | solution.py:189
  52.2 6.3 shard_map.83
  59.5 6.1 shard_map.82
  66.6 5.9 shard_map.81
  75.4 6.4 shard_map.80
  81.8 5.5 shard_map.84.refs_4_
  87.3 6.1 all-to-all-start.1
  96.2 23.4 %collective-permute-done.1.refs_2_ = f32[8,256,128]{2,1,0:T(8,128)S(1)} collective-permute-done((f32[8,256,128]{2,1,0:T(8,128)}, f32[8,256,128]{2,1,0:T(8,128)S(1)}, u32[]{:S(2)}, u32[]{:S(2)}) %collective-permute-start.1) | collective-permute-done | bytes 1048608 | tf_op jit(solution)/shard_map/ppermute | solution.py:419
  119.6 21.5 %collective-permute-done.2.refs_3_ = f32[8,256,128]{2,1,0:T(8,128)S(1)} collective-permute-done((f32[8,256,128]{2,1,0:T(8,128)}, f32[8,256,128]{2,1,0:T(8,128)S(1)}, u32[]{:S(2)}, u32[]{:S(2)}) %collective-permute-start.2) | collective-permute-done | bytes 1048608 | tf_op jit(solution)/shard_map/ppermute | solution.py:419
  141.1 5.8 shard_map.85.refs_4_
  146.9 40.2 %all-to-all-done.1 = f32[64,8,16,128]{3,2,1,0:T(8,128)} async-done(((f32[64,8,16,128]{3,2,1,0:T(8,128)}), f32[64,8,16,128]{3,2,1,0:T(8,128)}, u32[]{:S(2)}, u32[]{:S(2)}) %all-to-all-start.1) | async-done | bytes 4194336 | tf_op jit(solution)/shard_map/all_to_all | solution.py:513
  187.1 4.6 all-to-all-start
  198.9 85.5 %all-to-all-done = f32[64,8,16,128]{3,2,1,0:T(8,128)} async-done(((f32[64,8,16,128]{3,2,1,0:T(8,128)}), f32[64,8,16,128]{3,2,1,0:T(8,128)}, u32[]{:S(2)}, u32[]{:S(2)}) %all-to-all-start) | async-done | bytes 4194336 | tf_op jit(solution)/shard_map/all_to_all | solution.py:513
  291.2 17.5 %shard_map.86 = (f32[8,256,128]{2,1,0:T(8,128)S(1)}, f32[8,256,128]{2,1,0:T(8,128)}, f32[8,256,128]{2,1,0:T(8,128)}, f32[8,256,128]{2,1,0:T(8,128)}, f32[2,64,128]{2,1,0:T(8,128)S(1)}) custom-call(bf16[3,2,256,256]{3,2,1,0:T(8,128)(2,1)S(1)} %copy-done.36, bf16[3,256,256]{2,1,0:T(8,128)(2,1)S(1)} %copy-done.40, f32[8,8,128,128]{3,2,1,0:T(8,128)} %bitcast.2.field_ref, ...), custom_call_target="tpu_custom_call" | custom-call | flops 199999995904 | bytes 1024 | tf_op jit(solution)/shard_map/pallas_call | solution.py:358
  308.7 5.5 shard_map.87.refs_4_
  314.2 4.7 all-to-all-start.3
  320.3 12.0 %collective-permute-done.17.refs_3_ = f32[8,256,128]{2,1,0:T(8,128)} collective-permute-done((f32[8,256,128]{2,1,0:T(8,128)}, f32[8,256,128]{2,1,0:T(8,128)}, u32[]{:S(2)}, u32[]{:S(2)}) %collective-permute-start.17) | collective-permute-done | bytes 1048608 | tf_op jit(solution)/shard_map/ppermute | solution.py:419
  332.3 2.2 collective-permute-start.23
  334.5 21.3 %collective-permute-done.7.refs_2_ = f32[8,256,128]{2,1,0:T(8,128)} collective-permute-done((f32[8,256,128]{2,1,0:T(8,128)}, f32[8,256,128]{2,1,0:T(8,128)}, u32[]{:S(2)}, u32[]{:S(2)}) %collective-permute-start.7) | collective-permute-done | bytes 1048608 | tf_op jit(solution)/shard_map/ppermute | solution.py:419
  357.2 20.0 %collective-permute-done.8.refs_3_ = f32[8,256,128]{2,1,0:T(8,128)} collective-permute-done((f32[8,256,128]{2,1,0:T(8,128)}, f32[8,256,128]{2,1,0:T(8,128)}, u32[]{:S(2)}, u32[]{:S(2)}) %collective-permute-start.8) | collective-permute-done | bytes 1048608 | tf_op jit(solution)/shard_map/ppermute | solution.py:419
  377.2 2.2 collective-permute-start.26
  379.5 17.5 %shard_map.88 = (f32[8,256,128]{2,1,0:T(8,128)S(1)}, f32[8,256,128]{2,1,0:T(8,128)}, f32[8,256,128]{2,1,0:T(8,128)}, f32[8,256,128]{2,1,0:T(8,128)}, f32[2,64,128]{2,1,0:T(8,128)S(1)}) custom-call(bf16[3,2,256,256]{3,2,1,0:T(8,128)(2,1)S(1)} %copy-done.37, bf16[3,256,256]{2,1,0:T(8,128)(2,1)S(1)} %copy-done.41, f32[8,8,128,128]{3,2,1,0:T(8,128)} %bitcast.3.field_ref, ...), custom_call_target="tpu_custom_call" | custom-call | flops 199999995904 | bytes 1024 | tf_op jit(solution)/shard_map/pallas_call | solution.py:358
  397.0 8.4 %shard_map.89 = f32[64,8,16,128]{3,2,1,0:T(8,128)} custom-call(bf16[256,256]{1,0:T(8,128)(2,1)S(1)} %copy-done.11, f32[8,256,128]{2,1,0:T(8,128)S(1)} %copy-done.1, f32[8,256,128]{2,1,0:T(8,128)} %collective-permute-done.6.refs_1_, f32[8,256,128]{2,1,0:T(8,128)} %collective-permute-done.7.refs_2_, f32[8,256,128]{2,1,0:T(8,128)} %collective-permute-done.8.refs_3_, ...), custom_call_target="tpu_custom_call" | custom-call | flops 1024 | bytes 1024 | tf_op jit(solution)/shard_map/pallas_call | solution.py:286
  405.5 16.7 %collective-permute-done.23.refs_3_ = f32[8,256,128]{2,1,0:T(8,128)} collective-permute-done((f32[8,256,128]{2,1,0:T(8,128)}, f32[8,256,128]{2,1,0:T(8,128)}, u32[]{:S(2)}, u32[]{:S(2)}) %collective-permute-start.23) | collective-permute-done | bytes 1048608 | tf_op jit(solution)/shard_map/ppermute | solution.py:419
  424.3 4.7 all-to-all-start.2
  429.1 16.6 %collective-permute-done.25.refs_6_.refs_2_ = f32[8,256,128]{2,1,0:T(8,128)} collective-permute-done((f32[8,256,128]{2,1,0:T(8,128)}, f32[8,256,128]{2,1,0:T(8,128)}, u32[]{:S(2)}, u32[]{:S(2)}) %collective-permute-start.25) | collective-permute-done | bytes 1048608 | tf_op jit(solution)/shard_map/ppermute | solution.py:419
  445.6 21.5 %collective-permute-done.26.refs_7_.refs_3_ = f32[8,256,128]{2,1,0:T(8,128)} collective-permute-done((f32[8,256,128]{2,1,0:T(8,128)}, f32[8,256,128]{2,1,0:T(8,128)}, u32[]{:S(2)}, u32[]{:S(2)}) %collective-permute-start.26) | collective-permute-done | bytes 1048608 | tf_op jit(solution)/shard_map/ppermute | solution.py:419
  467.1 17.4 %shard_map.90 = (f32[8,256,128]{2,1,0:T(8,128)S(1)}, f32[8,256,128]{2,1,0:T(8,128)}, f32[8,256,128]{2,1,0:T(8,128)}, f32[8,256,128]{2,1,0:T(8,128)}, f32[2,64,128]{2,1,0:T(8,128)S(1)}) custom-call(bf16[3,2,256,256]{3,2,1,0:T(8,128)(2,1)S(1)} %copy-done.37, bf16[3,256,256]{2,1,0:T(8,128)(2,1)S(1)} %copy-done.41, f32[8,8,128,128]{3,2,1,0:T(8,128)} %bitcast.5.field_ref, ...), custom_call_target="tpu_custom_call" | custom-call | flops 199999995904 | bytes 1024 | tf_op jit(solution)/shard_map/pallas_call | solution.py:358
  488.1 2.5 collective-permute-done.19.refs_2_
  490.6 21.5 %collective-permute-done.20.refs_3_ = f32[8,256,128]{2,1,0:T(8,128)} collective-permute-done((f32[8,256,128]{2,1,0:T(8,128)}, f32[8,256,128]{2,1,0:T(8,128)}, u32[]{:S(2)}, u32[]{:S(2)}) %collective-permute-start.20) | collective-permute-done | bytes 1048608 | tf_op jit(solution)/shard_map/ppermute | solution.py:419
  512.1 10.4 %all-to-all-done.2 = f32[64,8,16,128]{3,2,1,0:T(8,128)} async-done(((f32[64,8,16,128]{3,2,1,0:T(8,128)}), f32[64,8,16,128]{3,2,1,0:T(8,128)}, u32[]{:S(2)}, u32[]{:S(2)}) %all-to-all-start.2) | async-done | bytes 4194336 | tf_op jit(solution)/shard_map/all_to_all | solution.py:513
  522.5 12.9 %collective-permute-done.28.refs_6_.refs_2_ = f32[8,256,128]{2,1,0:T(8,128)S(1)} collective-permute-done((f32[8,256,128]{2,1,0:T(8,128)}, f32[8,256,128]{2,1,0:T(8,128)S(1)}, u32[]{:S(2)}, u32[]{:S(2)}) %collective-permute-start.28) | collective-permute-done | bytes 1048608 | tf_op jit(solution)/shard_map/ppermute | solution.py:419
  535.4 18.8 %collective-permute-done.29.refs_7_.refs_3_ = f32[8,256,128]{2,1,0:T(8,128)S(1)} collective-permute-done((f32[8,256,128]{2,1,0:T(8,128)}, f32[8,256,128]{2,1,0:T(8,128)S(1)}, u32[]{:S(2)}, u32[]{:S(2)}) %collective-permute-start.29) | collective-permute-done | bytes 1048608 | tf_op jit(solution)/shard_map/ppermute | solution.py:419
  557.4 16.8 %shard_map.91 = (f32[8,256,128]{2,1,0:T(8,128)S(1)}, f32[8,256,128]{2,1,0:T(8,128)S(1)}, f32[8,256,128]{2,1,0:T(8,128)S(1)}, f32[8,256,128]{2,1,0:T(8,128)S(1)}, f32[2,64,128]{2,1,0:T(8,128)S(1)}) custom-call(bf16[3,2,256,256]{3,2,1,0:T(8,128)(2,1)S(1)} %copy-done.38, bf16[3,256,256]{2,1,0:T(8,128)(2,1)S(1)} %copy-done.42, ...), custom_call_target="tpu_custom_call" | custom-call | flops 199999995904 | bytes 1024 | tf_op jit(solution)/shard_map/pallas_call | solution.py:358
  578.7 22.3 %collective-permute-done.31.refs_2_.refs_5_ = f32[8,256,128]{2,1,0:T(8,128)S(1)} collective-permute-done((f32[8,256,128]{2,1,0:T(8,128)S(1)}, f32[8,256,128]{2,1,0:T(8,128)S(1)}, u32[]{:S(2)}, u32[]{:S(2)}) %collective-permute-start.31) | collective-permute-done | bytes 1048608 | tf_op jit(solution)/shard_map/ppermute | solution.py:419
  601.0 21.5 %collective-permute-done.32.refs_3_.refs_6_ = f32[8,256,128]{2,1,0:T(8,128)S(1)} collective-permute-done((f32[8,256,128]{2,1,0:T(8,128)S(1)}, f32[8,256,128]{2,1,0:T(8,128)S(1)}, u32[]{:S(2)}, u32[]{:S(2)}) %collective-permute-start.32) | collective-permute-done | bytes 1048608 | tf_op jit(solution)/shard_map/ppermute | solution.py:419
  625.0 2.2 collective-permute-start.37
  630.3 2.1 collective-permute-done.38
  632.4 2.4 collective-permute-start.39
  634.8 2.1 collective-permute-done.39
  638.3 6.5 shard_map.92.refs_4_
  645.9 20.7 %collective-permute-done.35.refs_3_ = f32[8,256,128]{2,1,0:T(8,128)S(1)} collective-permute-done((f32[8,256,128]{2,1,0:T(8,128)}, f32[8,256,128]{2,1,0:T(8,128)S(1)}, u32[]{:S(2)}, u32[]{:S(2)}) %collective-permute-start.35) | collective-permute-done | bytes 1048608 | tf_op jit(solution)/shard_map/ppermute | solution.py:419
  666.6 3.5 shard_map.93.refs_4_
  670.1 3.5 shard_map.94.refs_4_
  673.7 3.5 shard_map.95
  (157 shorter events, 57.8 us)
Async XLA Ops:
  8.0 133.2 %copy-start.9 = (bf16[256,256]{1,0:T(8,128)(2,1)}, bf16[256,256]{1,0:T(8,128)(2,1)S(1)}, u32[]{:S(2)}) copy-start(bf16[256,256]{1,0:T(8,128)(2,1)S(1)} %get-tuple-element.70.weight_ref) | copy-start | bytes 393220
  25.2 56.6 %collective-permute-start.3 = (f32[8,256,128]{2,1,0:T(8,128)S(1)}, f32[8,256,128]{2,1,0:T(8,128)S(1)}, u32[]{:S(2)}, u32[]{:S(2)}) collective-permute-start(f32[8,256,128]{2,1,0:T(8,128)S(1)} %get-tuple-element.81), channel_id=1, source_target_pairs={{0,8},{8,0},{16,24},{24,16},{1,9},{9,1},{17,25},{25,17},{2,10},{10... | collective-permute-start | bytes 3145736 | tf_op jit(solution)/shard_map/ppermute | solution.py:419
  25.7 56.1 %collective-permute-start.4 = (f32[8,256,128]{2,1,0:T(8,128)S(1)}, f32[8,256,128]{2,1,0:T(8,128)S(1)}, u32[]{:S(2)}, u32[]{:S(2)}) collective-permute-start(f32[8,256,128]{2,1,0:T(8,128)S(1)} %get-tuple-element.82), channel_id=1, source_target_pairs={{0,16},{8,24},{16,0},{24,8},{1,17},{9,25},{17,1},{25,9},{2,18},{10... | collective-permute-start | bytes 3145736 | tf_op jit(solution)/shard_map/ppermute | solution.py:419
  28.2 53.6 %collective-permute-start.5 = (f32[8,256,128]{2,1,0:T(8,128)S(1)}, f32[8,256,128]{2,1,0:T(8,128)S(1)}, u32[]{:S(2)}, u32[]{:S(2)}) collective-permute-start(f32[8,256,128]{2,1,0:T(8,128)S(1)} %get-tuple-element.83), channel_id=1, source_target_pairs={{0,24},{8,16},{16,8},{24,0},{1,25},{9,17},{17,9},{25,1},{2,26},{10... | collective-permute-start | bytes 3145736 | tf_op jit(solution)/shard_map/ppermute | solution.py:419
  87.3 99.8 %all-to-all-start.1 = ((f32[64,8,16,128]{3,2,1,0:T(8,128)}), f32[64,8,16,128]{3,2,1,0:T(8,128)}, u32[]{:S(2)}, u32[]{:S(2)}) async-start(f32[64,8,16,128]{3,2,1,0:T(8,128)} %shard_map.84.refs_4_), calls=%async_computation.1 | async-start | bytes 8388608 | tf_op jit(solution)/shard_map/all_to_all | solution.py:513
  93.3 2.9 collective-permute-start
  93.3 26.2 %collective-permute-start.1 = (f32[8,256,128]{2,1,0:T(8,128)}, f32[8,256,128]{2,1,0:T(8,128)S(1)}, u32[]{:S(2)}, u32[]{:S(2)}) collective-permute-start(f32[8,256,128]{2,1,0:T(8,128)} %copy-done.33), channel_id=1, source_target_pairs={{0,16},{8,24},{16,0},{24,8},{1,17},{9,25},{17,1},{25,9},{2,18},{10... | collective-permute-start | bytes 3145736 | tf_op jit(solution)/shard_map/ppermute | solution.py:419
  94.9 46.2 %collective-permute-start.2 = (f32[8,256,128]{2,1,0:T(8,128)}, f32[8,256,128]{2,1,0:T(8,128)S(1)}, u32[]{:S(2)}, u32[]{:S(2)}) collective-permute-start(f32[8,256,128]{2,1,0:T(8,128)} %copy-done.32), channel_id=1, source_target_pairs={{0,24},{8,16},{16,8},{24,0},{1,25},{9,17},{17,9},{25,1},{2,26},{10... | collective-permute-start | bytes 3145736 | tf_op jit(solution)/shard_map/ppermute | solution.py:419
  187.1 97.3 %all-to-all-start = ((f32[64,8,16,128]{3,2,1,0:T(8,128)}), f32[64,8,16,128]{3,2,1,0:T(8,128)}, u32[]{:S(2)}, u32[]{:S(2)}) async-start(f32[64,8,16,128]{3,2,1,0:T(8,128)} %shard_map.85.refs_4_), calls=%async_computation | async-start | bytes 8388608 | tf_op jit(solution)/shard_map/all_to_all | solution.py:513
  191.6 3.4 collective-permute-start.21
  191.7 4.5 collective-permute-start.15
  192.2 5.5 collective-permute-start.12
  192.3 92.1 %collective-permute-start.13 = (f32[8,256,128]{2,1,0:T(8,128)}, f32[8,256,128]{2,1,0:T(8,128)}, u32[]{:S(2)}, u32[]{:S(2)}) collective-permute-start(f32[8,256,128]{2,1,0:T(8,128)} %get-tuple-element.102), channel_id=1, source_target_pairs={{0,16},{8,24},{16,0},{24,8},{1,17},{9,25},{17,1},{25,9},{2,18},{10... | collective-permute-start | bytes 3145736 | tf_op jit(solution)/shard_map/ppermute | solution.py:419
  193.8 92.1 %collective-permute-start.14 = (f32[8,256,128]{2,1,0:T(8,128)}, f32[8,256,128]{2,1,0:T(8,128)}, u32[]{:S(2)}, u32[]{:S(2)}) collective-permute-start(f32[8,256,128]{2,1,0:T(8,128)} %get-tuple-element.103), channel_id=1, source_target_pairs={{0,24},{8,16},{16,8},{24,0},{1,25},{9,17},{17,9},{25,1},{2,26},{10... | collective-permute-start | bytes 3145736 | tf_op jit(solution)/shard_map/ppermute | solution.py:419
  195.1 90.8 %collective-permute-start.9 = (f32[8,256,128]{2,1,0:T(8,128)}, f32[8,256,128]{2,1,0:T(8,128)S(1)}, u32[]{:S(2)}, u32[]{:S(2)}) collective-permute-start(f32[8,256,128]{2,1,0:T(8,128)} %get-tuple-element.97), channel_id=1, source_target_pairs={{0,8},{8,0},{16,24},{24,16},{1,9},{9,1},{17,25},{25,17},{2,10},{10... | collective-permute-start | bytes 3145736 | tf_op jit(solution)/shard_map/ppermute | solution.py:419
  196.2 91.3 %collective-permute-start.10 = (f32[8,256,128]{2,1,0:T(8,128)}, f32[8,256,128]{2,1,0:T(8,128)S(1)}, u32[]{:S(2)}, u32[]{:S(2)}) collective-permute-start(f32[8,256,128]{2,1,0:T(8,128)} %get-tuple-element.98), channel_id=1, source_target_pairs={{0,16},{8,24},{16,0},{24,8},{1,17},{9,25},{17,1},{25,9},{2,18},{10... | collective-permute-start | bytes 3145736 | tf_op jit(solution)/shard_map/ppermute | solution.py:419
  197.7 91.3 %collective-permute-start.11 = (f32[8,256,128]{2,1,0:T(8,128)}, f32[8,256,128]{2,1,0:T(8,128)S(1)}, u32[]{:S(2)}, u32[]{:S(2)}) collective-permute-start(f32[8,256,128]{2,1,0:T(8,128)} %get-tuple-element.99), channel_id=1, source_target_pairs={{0,24},{8,16},{16,8},{24,0},{1,25},{9,17},{17,9},{25,1},{2,26},{10... | collective-permute-start | bytes 3145736 | tf_op jit(solution)/shard_map/ppermute | solution.py:419
  284.4 34.5 %collective-permute-start.16 = (f32[8,256,128]{2,1,0:T(8,128)}, f32[8,256,128]{2,1,0:T(8,128)}, u32[]{:S(2)}, u32[]{:S(2)}) collective-permute-start(f32[8,256,128]{2,1,0:T(8,128)} %copy-done.31), channel_id=1, source_target_pairs={{0,16},{8,24},{16,0},{24,8},{1,17},{9,25},{17,1},{25,9},{2,18},{10... | collective-permute-start | bytes 3145736 | tf_op jit(solution)/shard_map/ppermute | solution.py:419
  285.9 46.4 %collective-permute-start.17 = (f32[8,256,128]{2,1,0:T(8,128)}, f32[8,256,128]{2,1,0:T(8,128)}, u32[]{:S(2)}, u32[]{:S(2)}) collective-permute-start(f32[8,256,128]{2,1,0:T(8,128)} %copy-done.30), channel_id=1, source_target_pairs={{0,24},{8,16},{16,8},{24,0},{1,25},{9,17},{17,9},{25,1},{2,26},{10... | collective-permute-start | bytes 3145736 | tf_op jit(solution)/shard_map/ppermute | solution.py:419
  286.9 47.6 %collective-permute-start.6 = (f32[8,256,128]{2,1,0:T(8,128)}, f32[8,256,128]{2,1,0:T(8,128)}, u32[]{:S(2)}, u32[]{:S(2)}) collective-permute-start(f32[8,256,128]{2,1,0:T(8,128)} %get-tuple-element.89), channel_id=1, source_target_pairs={{0,8},{8,0},{16,24},{24,16},{1,9},{9,1},{17,25},{25,17},{2,10},{10... | collective-permute-start | bytes 3145736 | tf_op jit(solution)/shard_map/ppermute | solution.py:419
  287.5 68.2 %collective-permute-start.7 = (f32[8,256,128]{2,1,0:T(8,128)}, f32[8,256,128]{2,1,0:T(8,128)}, u32[]{:S(2)}, u32[]{:S(2)}) collective-permute-start(f32[8,256,128]{2,1,0:T(8,128)} %get-tuple-element.90), channel_id=1, source_target_pairs={{0,16},{8,24},{16,0},{24,8},{1,17},{9,25},{17,1},{25,9},{2,18},{10... | collective-permute-start | bytes 3145736 | tf_op jit(solution)/shard_map/ppermute | solution.py:419
  289.0 88.2 %collective-permute-start.8 = (f32[8,256,128]{2,1,0:T(8,128)}, f32[8,256,128]{2,1,0:T(8,128)}, u32[]{:S(2)}, u32[]{:S(2)}) collective-permute-start(f32[8,256,128]{2,1,0:T(8,128)} %get-tuple-element.91), channel_id=1, source_target_pairs={{0,24},{8,16},{16,8},{24,0},{1,25},{9,17},{17,9},{25,1},{2,26},{10... | collective-permute-start | bytes 3145736 | tf_op jit(solution)/shard_map/ppermute | solution.py:419
  314.2 65.3 %copy-start.41 = (bf16[3,256,256]{2,1,0:T(8,128)(2,1)S(1)}, bf16[3,256,256]{2,1,0:T(8,128)(2,1)}, u32[]{:S(2)}) copy-start(bf16[3,256,256]{2,1,0:T(8,128)(2,1)} %copy-done.39) | copy-start | bytes 1179652
  314.2 110.2 %all-to-all-start.3 = ((f32[64,8,16,128]{3,2,1,0:T(8,128)}), f32[64,8,16,128]{3,2,1,0:T(8,128)}, u32[]{:S(2)}, u32[]{:S(2)}) async-start(f32[64,8,16,128]{3,2,1,0:T(8,128)} %shard_map.87.refs_4_), calls=%async_computation.3 | async-start | bytes 8388608 | tf_op jit(solution)/shard_map/all_to_all | solution.py:513
  318.9 86.5 %collective-permute-start.22 = (f32[8,256,128]{2,1,0:T(8,128)}, f32[8,256,128]{2,1,0:T(8,128)}, u32[]{:S(2)}, u32[]{:S(2)}) collective-permute-start(f32[8,256,128]{2,1,0:T(8,128)} %get-tuple-element.114), channel_id=1, source_target_pairs={{0,16},{8,24},{16,0},{24,8},{1,17},{9,25},{17,1},{25,9},{2,18},{10... | collective-permute-start | bytes 3145736 | tf_op jit(solution)/shard_map/ppermute | solution.py:419
  332.3 89.9 %collective-permute-start.23 = (f32[8,256,128]{2,1,0:T(8,128)}, f32[8,256,128]{2,1,0:T(8,128)}, u32[]{:S(2)}, u32[]{:S(2)}) collective-permute-start(f32[8,256,128]{2,1,0:T(8,128)} %get-tuple-element.115), channel_id=1, source_target_pairs={{0,24},{8,16},{16,8},{24,0},{1,25},{9,17},{17,9},{25,1},{2,26},{10... | collective-permute-start | bytes 3145736 | tf_op jit(solution)/shard_map/ppermute | solution.py:419
  334.5 88.2 %collective-permute-start.24 = (f32[8,256,128]{2,1,0:T(8,128)}, f32[8,256,128]{2,1,0:T(8,128)}, u32[]{:S(2)}, u32[]{:S(2)}) collective-permute-start(f32[8,256,128]{2,1,0:T(8,128)} %get-tuple-element.116), channel_id=1, source_target_pairs={{0,8},{8,0},{16,24},{24,16},{1,9},{9,1},{17,25},{25,17},{2,10},{10... | collective-permute-start | bytes 3145736 | tf_op jit(solution)/shard_map/ppermute | solution.py:419
  355.8 89.9 %collective-permute-start.25 = (f32[8,256,128]{2,1,0:T(8,128)}, f32[8,256,128]{2,1,0:T(8,128)}, u32[]{:S(2)}, u32[]{:S(2)}) collective-permute-start(f32[8,256,128]{2,1,0:T(8,128)} %get-tuple-element.117), channel_id=1, source_target_pairs={{0,16},{8,24},{16,0},{24,8},{1,17},{9,25},{17,1},{25,9},{2,18},{10... | collective-permute-start | bytes 3145736 | tf_op jit(solution)/shard_map/ppermute | solution.py:419
  377.2 89.9 %collective-permute-start.26 = (f32[8,256,128]{2,1,0:T(8,128)}, f32[8,256,128]{2,1,0:T(8,128)}, u32[]{:S(2)}, u32[]{:S(2)}) collective-permute-start(f32[8,256,128]{2,1,0:T(8,128)} %get-tuple-element.118), channel_id=1, source_target_pairs={{0,24},{8,16},{16,8},{24,0},{1,25},{9,17},{17,9},{25,1},{2,26},{10... | collective-permute-start | bytes 3145736 | tf_op jit(solution)/shard_map/ppermute | solution.py:419
  405.4 82.6 %collective-permute-start.18 = (f32[8,256,128]{2,1,0:T(8,128)}, f32[8,256,128]{2,1,0:T(8,128)}, u32[]{:S(2)}, u32[]{:S(2)}) collective-permute-start(f32[8,256,128]{2,1,0:T(8,128)} %get-tuple-element.110), channel_id=1, source_target_pairs={{0,8},{8,0},{16,24},{24,16},{1,9},{9,1},{17,25},{25,17},{2,10},{10... | collective-permute-start | bytes 3145736 | tf_op jit(solution)/shard_map/ppermute | solution.py:419
  422.2 68.4 %collective-permute-start.19 = (f32[8,256,128]{2,1,0:T(8,128)}, f32[8,256,128]{2,1,0:T(8,128)}, u32[]{:S(2)}, u32[]{:S(2)}) collective-permute-start(f32[8,256,128]{2,1,0:T(8,128)} %get-tuple-element.111), channel_id=1, source_target_pairs={{0,16},{8,24},{16,0},{24,8},{1,17},{9,25},{17,1},{25,9},{2,18},{10... | collective-permute-start | bytes 3145736 | tf_op jit(solution)/shard_map/ppermute | solution.py:419
  422.7 89.3 %collective-permute-start.20 = (f32[8,256,128]{2,1,0:T(8,128)}, f32[8,256,128]{2,1,0:T(8,128)}, u32[]{:S(2)}, u32[]{:S(2)}) collective-permute-start(f32[8,256,128]{2,1,0:T(8,128)} %get-tuple-element.112), channel_id=1, source_target_pairs={{0,24},{8,16},{16,8},{24,0},{1,25},{9,17},{17,9},{25,1},{2,26},{10... | collective-permute-start | bytes 3145736 | tf_op jit(solution)/shard_map/ppermute | solution.py:419
  424.3 98.2 %all-to-all-start.2 = ((f32[64,8,16,128]{3,2,1,0:T(8,128)}), f32[64,8,16,128]{3,2,1,0:T(8,128)}, u32[]{:S(2)}, u32[]{:S(2)}) async-start(f32[64,8,16,128]{3,2,1,0:T(8,128)} %shard_map.89), calls=%async_computation.2 | async-start | bytes 8388608 | tf_op jit(solution)/shard_map/all_to_all | solution.py:513
  485.5 37.0 %collective-permute-start.27 = (f32[8,256,128]{2,1,0:T(8,128)}, f32[8,256,128]{2,1,0:T(8,128)S(1)}, u32[]{:S(2)}, u32[]{:S(2)}) collective-permute-start(f32[8,256,128]{2,1,0:T(8,128)} %get-tuple-element.120), channel_id=1, source_target_pairs={{0,8},{8,0},{16,24},{24,16},{1,9},{9,1},{17,25},{25,17},{2,10},{10... | collective-permute-start | bytes 3145736 | tf_op jit(solution)/shard_map/ppermute | solution.py:419
  486.6 48.8 %collective-permute-start.28 = (f32[8,256,128]{2,1,0:T(8,128)}, f32[8,256,128]{2,1,0:T(8,128)S(1)}, u32[]{:S(2)}, u32[]{:S(2)}) collective-permute-start(f32[8,256,128]{2,1,0:T(8,128)} %get-tuple-element.121), channel_id=1, source_target_pairs={{0,16},{8,24},{16,0},{24,8},{1,17},{9,25},{17,1},{25,9},{2,18},{10... | collective-permute-start | bytes 3145736 | tf_op jit(solution)/shard_map/ppermute | solution.py:419
  488.1 66.2 %collective-permute-start.29 = (f32[8,256,128]{2,1,0:T(8,128)}, f32[8,256,128]{2,1,0:T(8,128)S(1)}, u32[]{:S(2)}, u32[]{:S(2)}) collective-permute-start(f32[8,256,128]{2,1,0:T(8,128)} %get-tuple-element.122), channel_id=1, source_target_pairs={{0,24},{8,16},{16,8},{24,0},{1,25},{9,17},{17,9},{25,1},{2,26},{10... | collective-permute-start | bytes 3145736 | tf_op jit(solution)/shard_map/ppermute | solution.py:419
  557.4 80.9 %copy-start.6 = (f32[8,256,128]{2,1,0:T(8,128)S(1)}, f32[8,256,128]{2,1,0:T(8,128)}, u32[]{:S(2)}) copy-start(f32[8,256,128]{2,1,0:T(8,128)} %copy-done.5) | copy-start | bytes 3145732
  574.2 4.4 collective-permute-start.30
  574.9 26.0 %collective-permute-start.31 = (f32[8,256,128]{2,1,0:T(8,128)S(1)}, f32[8,256,128]{2,1,0:T(8,128)S(1)}, u32[]{:S(2)}, u32[]{:S(2)}) collective-permute-start(f32[8,256,128]{2,1,0:T(8,128)S(1)} %get-tuple-element.125), channel_id=1, source_target_pairs={{0,16},{8,24},{16,0},{24,8},{1,17},{9,25},{17,1},{25,9},{2,18},{10... | collective-permute-start | bytes 3145736 | tf_op jit(solution)/shard_map/ppermute | solution.py:419
  576.4 46.0 %collective-permute-start.32 = (f32[8,256,128]{2,1,0:T(8,128)S(1)}, f32[8,256,128]{2,1,0:T(8,128)S(1)}, u32[]{:S(2)}, u32[]{:S(2)}) collective-permute-start(f32[8,256,128]{2,1,0:T(8,128)S(1)} %get-tuple-element.126), channel_id=1, source_target_pairs={{0,24},{8,16},{16,8},{24,0},{1,25},{9,17},{17,9},{25,1},{2,26},{10... | collective-permute-start | bytes 3145736 | tf_op jit(solution)/shard_map/ppermute | solution.py:419
  576.4 68.4 %collective-permute-start.33 = (f32[8,256,128]{2,1,0:T(8,128)}, f32[8,256,128]{2,1,0:T(8,128)S(1)}, u32[]{:S(2)}, u32[]{:S(2)}) collective-permute-start(f32[8,256,128]{2,1,0:T(8,128)} %get-tuple-element.127), channel_id=1, source_target_pairs={{0,8},{8,0},{16,24},{24,16},{1,9},{9,1},{17,25},{25,17},{2,10},{10... | collective-permute-start | bytes 3145736 | tf_op jit(solution)/shard_map/ppermute | solution.py:419
  577.1 68.8 %collective-permute-start.34 = (f32[8,256,128]{2,1,0:T(8,128)}, f32[8,256,128]{2,1,0:T(8,128)S(1)}, u32[]{:S(2)}, u32[]{:S(2)}) collective-permute-start(f32[8,256,128]{2,1,0:T(8,128)} %get-tuple-element.128), channel_id=1, source_target_pairs={{0,16},{8,24},{16,0},{24,8},{1,17},{9,25},{17,1},{25,9},{2,18},{10... | collective-permute-start | bytes 3145736 | tf_op jit(solution)/shard_map/ppermute | solution.py:419
  578.6 88.1 %collective-permute-start.35 = (f32[8,256,128]{2,1,0:T(8,128)}, f32[8,256,128]{2,1,0:T(8,128)S(1)}, u32[]{:S(2)}, u32[]{:S(2)}) collective-permute-start(f32[8,256,128]{2,1,0:T(8,128)} %get-tuple-element.129), channel_id=1, source_target_pairs={{0,24},{8,16},{16,8},{24,0},{1,25},{9,17},{17,9},{25,1},{2,26},{10... | collective-permute-start | bytes 3145736 | tf_op jit(solution)/shard_map/ppermute | solution.py:419
  623.3 1.6 collective-permute-start.36
  625.0 3.8 collective-permute-start.37
  628.8 3.6 collective-permute-start.38
  632.4 4.5 collective-permute-start.39
  636.8 40.3 %collective-permute-start.40 = (f32[4,64]{1,0:T(4,128)S(1)}, f32[4,64]{1,0:T(4,128)S(1)}, u32[]{:S(2)}, u32[]{:S(2)}) collective-permute-start(f32[4,64]{1,0:T(4,128)S(1)} %add.18), channel_id=1, source_target_pairs={{0,16},{8,24},{16,0},{24,8},{1,17},{9,25},{17,1},{25,9},{2,18},{10... | collective-permute-start | bytes 3080 | tf_op jit(solution)/shard_map/ppermute | solution.py:463
  (41 other events, 401.6 us)

commit v2 on v1

--- a/solution.py
+++ b/solution.py
@@ -491,12 +491,9 @@
     shape = (2, rows // WIDE, parts, chunks, size, cols)
     fields, closed, made, grads = [], [], [], []
 
-    def close(chunk):
-        waited = closed[chunk - 1][:1] if chunk > 0 else []
-        if chunk == chunks - 1 and chunk > 0:
-            waited = waited + list(made[chunk - 1][1:])
-        elif chunk > 1:
-            waited = waited + list(made[chunk - 2][1:])
+    def close(chunk, waited):
+        if chunk > 0:
+            waited = waited + closed[chunk - 1][:1]
         out, grad = close_columns(
             fields[chunk], rho_there[chunk], lane, level, size, waited
         )
@@ -505,19 +502,24 @@
         grads.append(grad)
 
     for chunk in range(chunks):
-        waited = [pieces[0] for pieces in rho] if chunk == 0 else [field]
+        waited = [rho[chunk][0]]
+        if chunk > 0:
+            waited.append(field)
+        if chunk == 1:
+            waited += rho_there[0][1:]
         if chunk > 1:
-            close(chunk - 2)
-            waited = waited + closed[chunk - 2][:1]
+            close(chunk - 2, [])
+            waited += closed[chunk - 2][:1]
         field = turn_columns(state[chunk], turned_by, size, waited)
         fields.append(lax.all_to_all(field, "dev", split_axis=0, concat_axis=0, tiled=True))
         if chunk + 2 < chunks:
             pieces, fields[chunk] = lax.optimization_barrier((state_cut[chunk + 2], fields[chunk]))
             state.append(swap(pieces, parts))
-    for chunk in range(len(made), chunks):
-        close(chunk)
     whole = None
     for chunk in range(chunks):
+        if chunk == len(made):
+            waited = list(made[chunk - 2][1:]) if chunk > 1 else []
+            close(chunk, [whole] if 0 < chunk == chunks - 1 else waited)
         whole = place_pieces(made[chunk], seats, whole, chunk, shape, size)
     grad = grand_total(device_grad(grads, seats, parts, made[-1][1:]))
     return whole.reshape(costate.shape), grad.reshape(2, 2, LEVELS)

time: 680 us -> 689 us (1.013)
  waiting for transfers between devices: 420 us -> 427 us
    ppermute x36, waiting for transfers between devices: 277 us -> 341 us  [swap(): moved.append(lax.ppermute(pieces[step], 'grp', pairs))]
    all_to_all x4, waiting for transfers between devices: 136 us -> 77.4 us  [per_device(): lax.all_to_all(field, 'dev', split_axis=0, concat_axis=0, tiled=True)]
    unnamed x88 -> x80, local copies, waits for them, and re-layouts: 22.3 us -> 24.2 us
  transfers between devices with their start and end apart: 45 -> 45, of which waited for: 26 -> 25; matrix products, arithmetic and copies ran while one was open for 0% -> 0% of each run, Pallas kernels for 20% -> 19%
where the time goes in v2:
time: 689 us; the launch traced here: 686 us
  waiting for transfers between devices  427 us (62%)
  Pallas kernels  175 us (25%)
  starting transfers between devices  57.7 us (8%)
  local copies, waits for them, and re-layouts  24.2 us (4%)
    ppermute x36, waiting for transfers between devices, swap(): moved.append(lax.ppermute(pieces[step], 'grp', pairs))  341 us
    all_to_all x4, waiting for transfers between devices, per_device(): lax.all_to_all(field, 'dev', split_axis=0, concat_axis=0, tiled=True)  77.4 us
    pallas_call x4, Pallas kernels, close_columns(): pl.pallas_call(functools.partial(close_kernel, parts, size), grid=(firsts...  68.4 us
    pallas_call x2, Pallas kernels, open_state(): pl.pallas_call(functools.partial(open_kernel, count, len(waited)), grid=(...  34.9 us
    ppermute x36, starting transfers between devices, swap(): moved.append(lax.ppermute(pieces[step], 'grp', pairs))  30.5 us
    pallas_call x4, Pallas kernels, turn_columns(): pl.pallas_call(functools.partial(turn_kernel, parts, size), grid=(firsts,...  27 us
    unnamed x80, local copies, waits for them, and re-layouts  24.2 us
    pallas_call x4, Pallas kernels, cut_pieces(): pl.pallas_call(functools.partial(cut_kernel, size, len(waited)), grid=(fi...  21.5 us
  transfers between devices with their start and end apart: 45, of which 25 were waited for; matrix products, arithmetic and copies ran while one was open for 0% of the time, Pallas kernels for 19%

profile of v2, /device:TPU:0, one launch (start us, length us, event | category | flops | bytes accessed | tf_op | source)
XLA Modules:
  0.0 686.3 jit_solution(10329343255469058789)
XLA Ops:
  4.6 2.6 shard_map.77
  8.0 16.2 %shard_map.78 = (f32[8,256,128]{2,1,0:T(8,128)S(1)}, f32[8,256,128]{2,1,0:T(8,128)S(1)}, f32[8,256,128]{2,1,0:T(8,128)S(1)}, f32[8,256,128]{2,1,0:T(8,128)S(1)}) custom-call(bf16[2,64,256]{2,1,0:T(8,128)(2,1)S(1)} %slice.7.weight_ref, f32[2,1024,2048]{2,1,0:T(8,128)} %field_ref.3), custom_call_target="tpu_custom_call" | custom-call | flops 1024 | bytes 1024 | tf_op jit(solution)/shard_map/pallas_call | solution.py:189
  25.6 2.5 collective-permute-start.4
  28.3 18.7 %shard_map.79 = (f32[8,256,128]{2,1,0:T(8,128)S(1)}, f32[8,256,128]{2,1,0:T(8,128)S(1)}, f32[8,256,128]{2,1,0:T(8,128)S(1)}, f32[8,256,128]{2,1,0:T(8,128)S(1)},...) custom-call(bf16[2,192,256]{2,1,0:T(8,128)(2,1)S(1)} %slice.6.weight, ...), custom_call_target="tpu_custom_call" | custom-call | flops 1024 | bytes 1024 | tf_op jit(solution)/shard_map/pallas_call | solution.py:189
  51.2 4.7 shard_map.81
  58.9 15.3 %collective-permute-done.5.refs_3_ = f32[8,256,128]{2,1,0:T(8,128)S(1)} collective-permute-done((f32[8,256,128]{2,1,0:T(8,128)S(1)}, f32[8,256,128]{2,1,0:T(8,128)S(1)}, u32[]{:S(2)}, u32[]{:S(2)}) %collective-permute-start.5) | collective-permute-done | bytes 1048608 | tf_op jit(solution)/shard_map/ppermute | solution.py:419
  74.2 5.4 shard_map.82.refs_5_
  80.6 6.0 all-to-all-start.1
  90.8 5.9 shard_map.80
  98.6 14.3 %collective-permute-done.1.refs_2_ = f32[8,256,128]{2,1,0:T(8,128)S(1)} collective-permute-done((f32[8,256,128]{2,1,0:T(8,128)}, f32[8,256,128]{2,1,0:T(8,128)S(1)}, u32[]{:S(2)}, u32[]{:S(2)}) %collective-permute-start.1) | collective-permute-done | bytes 1048608 | tf_op jit(solution)/shard_map/ppermute | solution.py:419
  112.9 21.5 %collective-permute-done.2.refs_3_ = f32[8,256,128]{2,1,0:T(8,128)S(1)} collective-permute-done((f32[8,256,128]{2,1,0:T(8,128)S(1)}, f32[8,256,128]{2,1,0:T(8,128)S(1)}, u32[]{:S(2)}, u32[]{:S(2)}) %collective-permute-start.2) | collective-permute-done | bytes 1048608 | tf_op jit(solution)/shard_map/ppermute | solution.py:419
  134.4 23.4 %collective-permute-done.7.refs_7_.refs_2_ = f32[8,256,128]{2,1,0:T(8,128)S(1)} collective-permute-done((f32[8,256,128]{2,1,0:T(8,128)}, f32[8,256,128]{2,1,0:T(8,128)S(1)}, u32[]{:S(2)}, u32[]{:S(2)}) %collective-permute-start.7) | collective-permute-done | bytes 1048608 | tf_op jit(solution)/shard_map/ppermute | solution.py:419
  157.9 21.5 %collective-permute-done.8.refs_8_.refs_3_ = f32[8,256,128]{2,1,0:T(8,128)S(1)} collective-permute-done((f32[8,256,128]{2,1,0:T(8,128)}, f32[8,256,128]{2,1,0:T(8,128)S(1)}, u32[]{:S(2)}, u32[]{:S(2)}) %collective-permute-start.8) | collective-permute-done | bytes 1048608 | tf_op jit(solution)/shard_map/ppermute | solution.py:419
  180.4 5.6 shard_map.83.refs_5_
  187.0 6.1 all-to-all-start
  193.0 6.3 shard_map.85
  201.7 4.6 shard_map.84
  209.3 77.4 %all-to-all-done = f32[64,8,16,128]{3,2,1,0:T(8,128)} async-done(((f32[64,8,16,128]{3,2,1,0:T(8,128)}), f32[64,8,16,128]{3,2,1,0:T(8,128)}, u32[]{:S(2)}, u32[]{:S(2)}) %all-to-all-start) | async-done | bytes 4194336 | tf_op jit(solution)/shard_map/all_to_all | solution.py:514
  292.5 17.5 %shard_map.86 = (f32[8,256,128]{2,1,0:T(8,128)S(1)}, f32[8,256,128]{2,1,0:T(8,128)}, f32[8,256,128]{2,1,0:T(8,128)}, f32[8,256,128]{2,1,0:T(8,128)}, f32[2,64,128]{2,1,0:T(8,128)S(1)}) custom-call(bf16[3,2,256,256]{3,2,1,0:T(8,128)(2,1)S(1)} %copy-done.32, bf16[3,256,256]{2,1,0:T(8,128)(2,1)S(1)} %copy-done.35, f32[8,8,128,128]{3,2,1,0:T(8,128)} %bitcast.2.field_ref, ...), custom_call_target="tpu_custom_call" | custom-call | flops 199999995904 | bytes 1024 | tf_op jit(solution)/shard_map/pallas_call | solution.py:358
  311.0 7.9 %shard_map.87.refs_5_ = f32[64,8,16,128]{3,2,1,0:T(8,128)} custom-call(bf16[256,256]{1,0:T(8,128)(2,1)S(1)} %get-tuple-element.70.weight_ref, f32[8,256,128]{2,1,0:T(8,128)S(1)} %copy-done.12, f32[8,256,128]{2,1,0:T(8,128)} %collective-permute-done.12.refs_1_, f32[8,256,128]{2,1,0:T(8,128)} %collective-permute-done.13.refs_2_, ...), custom_call_target="tpu_custom_call" | custom-call | flops 1024 | bytes 1024 | tf_op jit(solution)/shard_map/pallas_call | solution.py:286
  318.9 4.7 all-to-all-start.3
  325.1 9.5 %collective-permute-done.17.refs_3_ = f32[8,256,128]{2,1,0:T(8,128)} collective-permute-done((f32[8,256,128]{2,1,0:T(8,128)}, f32[8,256,128]{2,1,0:T(8,128)}, u32[]{:S(2)}, u32[]{:S(2)}) %collective-permute-start.17) | collective-permute-done | bytes 1048608 | tf_op jit(solution)/shard_map/ppermute | solution.py:419
  334.6 2.2 collective-permute-start.23
  336.8 21.3 %collective-permute-done.10.refs_2_ = f32[8,256,128]{2,1,0:T(8,128)} collective-permute-done((f32[8,256,128]{2,1,0:T(8,128)}, f32[8,256,128]{2,1,0:T(8,128)}, u32[]{:S(2)}, u32[]{:S(2)}) %collective-permute-start.10) | collective-permute-done | bytes 1048608 | tf_op jit(solution)/shard_map/ppermute | solution.py:419
  359.5 20.0 %collective-permute-done.11.refs_3_ = f32[8,256,128]{2,1,0:T(8,128)} collective-permute-done((f32[8,256,128]{2,1,0:T(8,128)}, f32[8,256,128]{2,1,0:T(8,128)}, u32[]{:S(2)}, u32[]{:S(2)}) %collective-permute-start.11) | collective-permute-done | bytes 1048608 | tf_op jit(solution)/shard_map/ppermute | solution.py:419
  379.5 2.2 collective-permute-start.26
  381.7 17.4 %shard_map.88 = (f32[8,256,128]{2,1,0:T(8,128)S(1)}, f32[8,256,128]{2,1,0:T(8,128)}, f32[8,256,128]{2,1,0:T(8,128)}, f32[8,256,128]{2,1,0:T(8,128)}, f32[2,64,128]{2,1,0:T(8,128)S(1)}) custom-call(bf16[3,2,256,256]{3,2,1,0:T(8,128)(2,1)S(1)} %copy-done.33, bf16[3,256,256]{2,1,0:T(8,128)(2,1)S(1)} %copy-done.36, f32[8,8,128,128]{3,2,1,0:T(8,128)} %bitcast.3.field_ref, ...), custom_call_target="tpu_custom_call" | custom-call | flops 199999995904 | bytes 1024 | tf_op jit(solution)/shard_map/pallas_call | solution.py:358
  400.1 8.1 %shard_map.89 = f32[64,8,16,128]{3,2,1,0:T(8,128)} custom-call(bf16[256,256]{1,0:T(8,128)(2,1)S(1)} %get-tuple-element.70.weight_ref, f32[8,256,128]{2,1,0:T(8,128)S(1)} %copy-done.1, f32[8,256,128]{2,1,0:T(8,128)} %collective-permute-done.9.refs_1_, f32[8,256,128]{2,1,0:T(8,128)} %collective-permute-done.10.refs_2_, ...), custom_call_target="tpu_custom_call" | custom-call | flops 1024 | bytes 1024 | tf_op jit(solution)/shard_map/pallas_call | solution.py:286
  408.2 16.3 %collective-permute-done.23.refs_3_ = f32[8,256,128]{2,1,0:T(8,128)} collective-permute-done((f32[8,256,128]{2,1,0:T(8,128)}, f32[8,256,128]{2,1,0:T(8,128)}, u32[]{:S(2)}, u32[]{:S(2)}) %collective-permute-start.23) | collective-permute-done | bytes 1048608 | tf_op jit(solution)/shard_map/ppermute | solution.py:419
  426.6 4.7 all-to-all-start.2
  431.4 16.6 %collective-permute-done.25.refs_5_.refs_2_ = f32[8,256,128]{2,1,0:T(8,128)} collective-permute-done((f32[8,256,128]{2,1,0:T(8,128)}, f32[8,256,128]{2,1,0:T(8,128)}, u32[]{:S(2)}, u32[]{:S(2)}) %collective-permute-start.25) | collective-permute-done | bytes 1048608 | tf_op jit(solution)/shard_map/ppermute | solution.py:419
  447.9 21.5 %collective-permute-done.26.refs_6_.refs_3_ = f32[8,256,128]{2,1,0:T(8,128)} collective-permute-done((f32[8,256,128]{2,1,0:T(8,128)}, f32[8,256,128]{2,1,0:T(8,128)}, u32[]{:S(2)}, u32[]{:S(2)}) %collective-permute-start.26) | collective-permute-done | bytes 1048608 | tf_op jit(solution)/shard_map/ppermute | solution.py:419
  469.4 16.8 %shard_map.90 = (f32[8,256,128]{2,1,0:T(8,128)S(1)}, f32[8,256,128]{2,1,0:T(8,128)S(1)}, f32[8,256,128]{2,1,0:T(8,128)S(1)}, f32[8,256,128]{2,1,0:T(8,128)S(1)}, f32[2,64,128]{2,1,0:T(8,128)S(1)}) custom-call(bf16[3,2,256,256]{3,2,1,0:T(8,128)(2,1)S(1)} %copy-done.33, bf16[3,256,256]{2,1,0:T(8,128)(2,1)S(1)} %copy-done.36, ...), custom_call_target="tpu_custom_call" | custom-call | flops 199999995904 | bytes 1024 | tf_op jit(solution)/shard_map/pallas_call | solution.py:358
  489.0 3.8 collective-permute-done.31.refs_2_
  492.9 21.5 %collective-permute-done.32.refs_3_ = f32[8,256,128]{2,1,0:T(8,128)} collective-permute-done((f32[8,256,128]{2,1,0:T(8,128)}, f32[8,256,128]{2,1,0:T(8,128)}, u32[]{:S(2)}, u32[]{:S(2)}) %collective-permute-start.32) | collective-permute-done | bytes 1048608 | tf_op jit(solution)/shard_map/ppermute | solution.py:419
  516.9 6.5 shard_map.91.refs_4_
  523.3 6.5 shard_map.92.refs_4_
  529.8 7.9 %collective-permute-done.28.refs_2_ = f32[8,256,128]{2,1,0:T(8,128)S(1)} collective-permute-done((f32[8,256,128]{2,1,0:T(8,128)S(1)}, f32[8,256,128]{2,1,0:T(8,128)S(1)}, u32[]{:S(2)}, u32[]{:S(2)}) %collective-permute-start.28) | collective-permute-done | bytes 1048608 | tf_op jit(solution)/shard_map/ppermute | solution.py:419
  537.7 21.5 %collective-permute-done.29.refs_3_ = f32[8,256,128]{2,1,0:T(8,128)S(1)} collective-permute-done((f32[8,256,128]{2,1,0:T(8,128)S(1)}, f32[8,256,128]{2,1,0:T(8,128)S(1)}, u32[]{:S(2)}, u32[]{:S(2)}) %collective-permute-start.29) | collective-permute-done | bytes 1048608 | tf_op jit(solution)/shard_map/ppermute | solution.py:419
  559.2 3.5 shard_map.93.refs_4_
  562.7 20.1 %collective-permute-done.19.refs_2_ = f32[8,256,128]{2,1,0:T(8,128)} collective-permute-done((f32[8,256,128]{2,1,0:T(8,128)S(1)}, f32[8,256,128]{2,1,0:T(8,128)}, u32[]{:S(2)}, u32[]{:S(2)}) %collective-permute-start.19) | collective-permute-done | bytes 1048608 | tf_op jit(solution)/shard_map/ppermute | solution.py:419
  582.8 19.5 %collective-permute-done.20.refs_3_ = f32[8,256,128]{2,1,0:T(8,128)} collective-permute-done((f32[8,256,128]{2,1,0:T(8,128)S(1)}, f32[8,256,128]{2,1,0:T(8,128)}, u32[]{:S(2)}, u32[]{:S(2)}) %collective-permute-start.20) | collective-permute-done | bytes 1048608 | tf_op jit(solution)/shard_map/ppermute | solution.py:419
  602.2 16.7 %shard_map.94 = (f32[8,256,128]{2,1,0:T(8,128)S(1)}, f32[8,256,128]{2,1,0:T(8,128)S(1)}, f32[8,256,128]{2,1,0:T(8,128)S(1)}, f32[8,256,128]{2,1,0:T(8,128)S(1)}, f32[2,64,128]{2,1,0:T(8,128)S(1)}) custom-call(bf16[3,2,256,256]{3,2,1,0:T(8,128)(2,1)S(1)} %copy-done.33, bf16[3,256,256]{2,1,0:T(8,128)(2,1)S(1)} %copy-done.36, ...), custom_call_target="tpu_custom_call" | custom-call | flops 199999995904 | bytes 1024 | tf_op jit(solution)/shard_map/pallas_call | solution.py:358
  622.2 23.7 %collective-permute-done.34.refs_2_.refs_5_ = f32[8,256,128]{2,1,0:T(8,128)S(1)} collective-permute-done((f32[8,256,128]{2,1,0:T(8,128)S(1)}, f32[8,256,128]{2,1,0:T(8,128)S(1)}, u32[]{:S(2)}, u32[]{:S(2)}) %collective-permute-start.34) | collective-permute-done | bytes 1048608 | tf_op jit(solution)/shard_map/ppermute | solution.py:419
  645.9 20.7 %collective-permute-done.35.refs_3_.refs_6_ = f32[8,256,128]{2,1,0:T(8,128)S(1)} collective-permute-done((f32[8,256,128]{2,1,0:T(8,128)S(1)}, f32[8,256,128]{2,1,0:T(8,128)S(1)}, u32[]{:S(2)}, u32[]{:S(2)}) %collective-permute-start.35) | collective-permute-done | bytes 1048608 | tf_op jit(solution)/shard_map/ppermute | solution.py:419
  673.0 3.2 collective-permute-done.38
  677.9 2.8 collective-permute-done.39
  682.2 3.5 shard_map.95
  (149 shorter events, 58.8 us)
Async XLA Ops:
  25.2 33.7 %collective-permute-start.3 = (f32[8,256,128]{2,1,0:T(8,128)S(1)}, f32[8,256,128]{2,1,0:T(8,128)S(1)}, u32[]{:S(2)}, u32[]{:S(2)}) collective-permute-start(f32[8,256,128]{2,1,0:T(8,128)S(1)} %get-tuple-element.82), channel_id=1, source_target_pairs={{0,8},{8,0},{16,24},{24,16},{1,9},{9,1},{17,25},{25,17},{2,10},{10... | collective-permute-start | bytes 3145736 | tf_op jit(solution)/shard_map/ppermute | solution.py:419
  25.6 33.3 %collective-permute-start.4 = (f32[8,256,128]{2,1,0:T(8,128)S(1)}, f32[8,256,128]{2,1,0:T(8,128)S(1)}, u32[]{:S(2)}, u32[]{:S(2)}) collective-permute-start(f32[8,256,128]{2,1,0:T(8,128)S(1)} %get-tuple-element.83), channel_id=1, source_target_pairs={{0,16},{8,24},{16,0},{24,8},{1,17},{9,25},{17,1},{25,9},{2,18},{10... | collective-permute-start | bytes 3145736 | tf_op jit(solution)/shard_map/ppermute | solution.py:419
  28.1 46.1 %collective-permute-start.5 = (f32[8,256,128]{2,1,0:T(8,128)S(1)}, f32[8,256,128]{2,1,0:T(8,128)S(1)}, u32[]{:S(2)}, u32[]{:S(2)}) collective-permute-start(f32[8,256,128]{2,1,0:T(8,128)S(1)} %get-tuple-element.84), channel_id=1, source_target_pairs={{0,24},{8,16},{16,8},{24,0},{1,25},{9,17},{17,9},{25,1},{2,26},{10... | collective-permute-start | bytes 3145736 | tf_op jit(solution)/shard_map/ppermute | solution.py:419
  80.6 106.3 %all-to-all-start.1 = ((f32[64,8,16,128]{3,2,1,0:T(8,128)}), f32[64,8,16,128]{3,2,1,0:T(8,128)}, u32[]{:S(2)}, u32[]{:S(2)}) async-start(f32[64,8,16,128]{3,2,1,0:T(8,128)} %shard_map.82.refs_5_), calls=%async_computation.1 | async-start | bytes 8388608 | tf_op jit(solution)/shard_map/all_to_all | solution.py:514
  86.7 3.7 collective-permute-start
  86.7 26.2 %collective-permute-start.1 = (f32[8,256,128]{2,1,0:T(8,128)}, f32[8,256,128]{2,1,0:T(8,128)S(1)}, u32[]{:S(2)}, u32[]{:S(2)}) collective-permute-start(f32[8,256,128]{2,1,0:T(8,128)} %copy-done.26), channel_id=1, source_target_pairs={{0,16},{8,24},{16,0},{24,8},{1,17},{9,25},{17,1},{25,9},{2,18},{10... | collective-permute-start | bytes 3145736 | tf_op jit(solution)/shard_map/ppermute | solution.py:419
  88.2 46.2 %collective-permute-start.2 = (f32[8,256,128]{2,1,0:T(8,128)S(1)}, f32[8,256,128]{2,1,0:T(8,128)S(1)}, u32[]{:S(2)}, u32[]{:S(2)}) collective-permute-start(f32[8,256,128]{2,1,0:T(8,128)S(1)} %get-tuple-element.80), channel_id=1, source_target_pairs={{0,24},{8,16},{16,8},{24,0},{1,25},{9,17},{17,9},{25,1},{2,26},{10... | collective-permute-start | bytes 3145736 | tf_op jit(solution)/shard_map/ppermute | solution.py:419
  88.5 45.9 %collective-permute-start.6 = (f32[8,256,128]{2,1,0:T(8,128)}, f32[8,256,128]{2,1,0:T(8,128)S(1)}, u32[]{:S(2)}, u32[]{:S(2)}) collective-permute-start(f32[8,256,128]{2,1,0:T(8,128)} %copy-done.29), channel_id=1, source_target_pairs={{0,8},{8,0},{16,24},{24,16},{1,9},{9,1},{17,25},{25,17},{2,10},{10... | collective-permute-start | bytes 3145736 | tf_op jit(solution)/shard_map/ppermute | solution.py:419
  88.9 69.0 %collective-permute-start.7 = (f32[8,256,128]{2,1,0:T(8,128)}, f32[8,256,128]{2,1,0:T(8,128)S(1)}, u32[]{:S(2)}, u32[]{:S(2)}) collective-permute-start(f32[8,256,128]{2,1,0:T(8,128)} %copy-done.28), channel_id=1, source_target_pairs={{0,16},{8,24},{16,0},{24,8},{1,17},{9,25},{17,1},{25,9},{2,18},{10... | collective-permute-start | bytes 3145736 | tf_op jit(solution)/shard_map/ppermute | solution.py:419
  90.4 89.0 %collective-permute-start.8 = (f32[8,256,128]{2,1,0:T(8,128)}, f32[8,256,128]{2,1,0:T(8,128)S(1)}, u32[]{:S(2)}, u32[]{:S(2)}) collective-permute-start(f32[8,256,128]{2,1,0:T(8,128)} %copy-done.27), channel_id=1, source_target_pairs={{0,24},{8,16},{16,8},{24,0},{1,25},{9,17},{17,9},{25,1},{2,26},{10... | collective-permute-start | bytes 3145736 | tf_op jit(solution)/shard_map/ppermute | solution.py:419
  187.0 99.7 %all-to-all-start = ((f32[64,8,16,128]{3,2,1,0:T(8,128)}), f32[64,8,16,128]{3,2,1,0:T(8,128)}, u32[]{:S(2)}, u32[]{:S(2)}) async-start(f32[64,8,16,128]{3,2,1,0:T(8,128)} %shard_map.83.refs_5_), calls=%async_computation | async-start | bytes 8388608 | tf_op jit(solution)/shard_map/all_to_all | solution.py:514
  199.3 111.7 %copy-start.10 = (f32[8,256,128]{2,1,0:T(8,128)}, f32[8,256,128]{2,1,0:T(8,128)S(1)}, u32[]{:S(2)}) copy-start(f32[8,256,128]{2,1,0:T(8,128)S(1)} %get-tuple-element.102.refs_4_.refs_0_) | copy-start | bytes 3145732
  199.3 87.4 %collective-permute-start.21 = (f32[8,256,128]{2,1,0:T(8,128)}, f32[8,256,128]{2,1,0:T(8,128)}, u32[]{:S(2)}, u32[]{:S(2)}) collective-permute-start(f32[8,256,128]{2,1,0:T(8,128)} %get-tuple-element.113), channel_id=1, source_target_pairs={{0,8},{8,0},{16,24},{24,16},{1,9},{9,1},{17,25},{25,17},{2,10},{10... | collective-permute-start | bytes 3145736 | tf_op jit(solution)/shard_map/ppermute | solution.py:419
  199.3 88.8 %collective-permute-start.15 = (f32[8,256,128]{2,1,0:T(8,128)}, f32[8,256,128]{2,1,0:T(8,128)}, u32[]{:S(2)}, u32[]{:S(2)}) collective-permute-start(f32[8,256,128]{2,1,0:T(8,128)} %get-tuple-element.106), channel_id=1, source_target_pairs={{0,8},{8,0},{16,24},{24,16},{1,9},{9,1},{17,25},{25,17},{2,10},{10... | collective-permute-start | bytes 3145736 | tf_op jit(solution)/shard_map/ppermute | solution.py:419
  199.9 88.3 %collective-permute-start.12 = (f32[8,256,128]{2,1,0:T(8,128)}, f32[8,256,128]{2,1,0:T(8,128)}, u32[]{:S(2)}, u32[]{:S(2)}) collective-permute-start(f32[8,256,128]{2,1,0:T(8,128)} %get-tuple-element.99), channel_id=1, source_target_pairs={{0,8},{8,0},{16,24},{24,16},{1,9},{9,1},{17,25},{25,17},{2,10},{10... | collective-permute-start | bytes 3145736 | tf_op jit(solution)/shard_map/ppermute | solution.py:419
  199.9 88.9 %collective-permute-start.13 = (f32[8,256,128]{2,1,0:T(8,128)}, f32[8,256,128]{2,1,0:T(8,128)}, u32[]{:S(2)}, u32[]{:S(2)}) collective-permute-start(f32[8,256,128]{2,1,0:T(8,128)} %get-tuple-element.100), channel_id=1, source_target_pairs={{0,16},{8,24},{16,0},{24,8},{1,17},{9,25},{17,1},{25,9},{2,18},{10... | collective-permute-start | bytes 3145736 | tf_op jit(solution)/shard_map/ppermute | solution.py:419
  201.4 88.9 %collective-permute-start.14 = (f32[8,256,128]{2,1,0:T(8,128)}, f32[8,256,128]{2,1,0:T(8,128)}, u32[]{:S(2)}, u32[]{:S(2)}) collective-permute-start(f32[8,256,128]{2,1,0:T(8,128)} %get-tuple-element.101), channel_id=1, source_target_pairs={{0,24},{8,16},{16,8},{24,0},{1,25},{9,17},{17,9},{25,1},{2,26},{10... | collective-permute-start | bytes 3145736 | tf_op jit(solution)/shard_map/ppermute | solution.py:419
  209.3 190.8 %copy-start.9 = (f32[8,256,128]{2,1,0:T(8,128)}, f32[8,256,128]{2,1,0:T(8,128)S(1)}, u32[]{:S(2)}) copy-start(f32[8,256,128]{2,1,0:T(8,128)S(1)} %get-tuple-element.93.refs_4_.refs_0_) | copy-start | bytes 3145732
  286.7 36.9 %collective-permute-start.16 = (f32[8,256,128]{2,1,0:T(8,128)}, f32[8,256,128]{2,1,0:T(8,128)}, u32[]{:S(2)}, u32[]{:S(2)}) collective-permute-start(f32[8,256,128]{2,1,0:T(8,128)} %copy-done.25), channel_id=1, source_target_pairs={{0,16},{8,24},{16,0},{24,8},{1,17},{9,25},{17,1},{25,9},{2,18},{10... | collective-permute-start | bytes 3145736 | tf_op jit(solution)/shard_map/ppermute | solution.py:419
  288.2 46.4 %collective-permute-start.17 = (f32[8,256,128]{2,1,0:T(8,128)}, f32[8,256,128]{2,1,0:T(8,128)}, u32[]{:S(2)}, u32[]{:S(2)}) collective-permute-start(f32[8,256,128]{2,1,0:T(8,128)} %copy-done.24), channel_id=1, source_target_pairs={{0,24},{8,16},{16,8},{24,0},{1,25},{9,17},{17,9},{25,1},{2,26},{10... | collective-permute-start | bytes 3145736 | tf_op jit(solution)/shard_map/ppermute | solution.py:419
  288.2 48.6 %collective-permute-start.9 = (f32[8,256,128]{2,1,0:T(8,128)}, f32[8,256,128]{2,1,0:T(8,128)}, u32[]{:S(2)}, u32[]{:S(2)}) collective-permute-start(f32[8,256,128]{2,1,0:T(8,128)} %get-tuple-element.90), channel_id=1, source_target_pairs={{0,8},{8,0},{16,24},{24,16},{1,9},{9,1},{17,25},{25,17},{2,10},{10... | collective-permute-start | bytes 3145736 | tf_op jit(solution)/shard_map/ppermute | solution.py:419
  288.9 69.2 %collective-permute-start.10 = (f32[8,256,128]{2,1,0:T(8,128)}, f32[8,256,128]{2,1,0:T(8,128)}, u32[]{:S(2)}, u32[]{:S(2)}) collective-permute-start(f32[8,256,128]{2,1,0:T(8,128)} %get-tuple-element.91), channel_id=1, source_target_pairs={{0,16},{8,24},{16,0},{24,8},{1,17},{9,25},{17,1},{25,9},{2,18},{10... | collective-permute-start | bytes 3145736 | tf_op jit(solution)/shard_map/ppermute | solution.py:419
  290.3 89.2 %collective-permute-start.11 = (f32[8,256,128]{2,1,0:T(8,128)}, f32[8,256,128]{2,1,0:T(8,128)}, u32[]{:S(2)}, u32[]{:S(2)}) collective-permute-start(f32[8,256,128]{2,1,0:T(8,128)} %get-tuple-element.92), channel_id=1, source_target_pairs={{0,24},{8,16},{16,8},{24,0},{1,25},{9,17},{17,9},{25,1},{2,26},{10... | collective-permute-start | bytes 3145736 | tf_op jit(solution)/shard_map/ppermute | solution.py:419
  318.9 107.7 %all-to-all-start.3 = ((f32[64,8,16,128]{3,2,1,0:T(8,128)}), f32[64,8,16,128]{3,2,1,0:T(8,128)}, u32[]{:S(2)}, u32[]{:S(2)}) async-start(f32[64,8,16,128]{3,2,1,0:T(8,128)} %shard_map.87.refs_5_), calls=%async_computation.3 | async-start | bytes 8388608 | tf_op jit(solution)/shard_map/all_to_all | solution.py:514
  323.6 84.5 %collective-permute-start.22 = (f32[8,256,128]{2,1,0:T(8,128)}, f32[8,256,128]{2,1,0:T(8,128)}, u32[]{:S(2)}, u32[]{:S(2)}) collective-permute-start(f32[8,256,128]{2,1,0:T(8,128)} %get-tuple-element.114), channel_id=1, source_target_pairs={{0,16},{8,24},{16,0},{24,8},{1,17},{9,25},{17,1},{25,9},{2,18},{10... | collective-permute-start | bytes 3145736 | tf_op jit(solution)/shard_map/ppermute | solution.py:419
  334.6 89.9 %collective-permute-start.23 = (f32[8,256,128]{2,1,0:T(8,128)}, f32[8,256,128]{2,1,0:T(8,128)}, u32[]{:S(2)}, u32[]{:S(2)}) collective-permute-start(f32[8,256,128]{2,1,0:T(8,128)} %get-tuple-element.115), channel_id=1, source_target_pairs={{0,24},{8,16},{16,8},{24,0},{1,25},{9,17},{17,9},{25,1},{2,26},{10... | collective-permute-start | bytes 3145736 | tf_op jit(solution)/shard_map/ppermute | solution.py:419
  336.8 88.2 %collective-permute-start.24 = (f32[8,256,128]{2,1,0:T(8,128)}, f32[8,256,128]{2,1,0:T(8,128)}, u32[]{:S(2)}, u32[]{:S(2)}) collective-permute-start(f32[8,256,128]{2,1,0:T(8,128)} %get-tuple-element.116), channel_id=1, source_target_pairs={{0,8},{8,0},{16,24},{24,16},{1,9},{9,1},{17,25},{25,17},{2,10},{10... | collective-permute-start | bytes 3145736 | tf_op jit(solution)/shard_map/ppermute | solution.py:419
  358.1 89.9 %collective-permute-start.25 = (f32[8,256,128]{2,1,0:T(8,128)}, f32[8,256,128]{2,1,0:T(8,128)}, u32[]{:S(2)}, u32[]{:S(2)}) collective-permute-start(f32[8,256,128]{2,1,0:T(8,128)} %get-tuple-element.117), channel_id=1, source_target_pairs={{0,16},{8,24},{16,0},{24,8},{1,17},{9,25},{17,1},{25,9},{2,18},{10... | collective-permute-start | bytes 3145736 | tf_op jit(solution)/shard_map/ppermute | solution.py:419
  379.5 89.9 %collective-permute-start.26 = (f32[8,256,128]{2,1,0:T(8,128)}, f32[8,256,128]{2,1,0:T(8,128)}, u32[]{:S(2)}, u32[]{:S(2)}) collective-permute-start(f32[8,256,128]{2,1,0:T(8,128)} %get-tuple-element.118), channel_id=1, source_target_pairs={{0,24},{8,16},{16,8},{24,0},{1,25},{9,17},{17,9},{25,1},{2,26},{10... | collective-permute-start | bytes 3145736 | tf_op jit(solution)/shard_map/ppermute | solution.py:419
  408.2 79.4 %collective-permute-start.30 = (f32[8,256,128]{2,1,0:T(8,128)}, f32[8,256,128]{2,1,0:T(8,128)}, u32[]{:S(2)}, u32[]{:S(2)}) collective-permute-start(f32[8,256,128]{2,1,0:T(8,128)} %get-tuple-element.123), channel_id=1, source_target_pairs={{0,8},{8,0},{16,24},{24,16},{1,9},{9,1},{17,25},{25,17},{2,10},{10... | collective-permute-start | bytes 3145736 | tf_op jit(solution)/shard_map/ppermute | solution.py:419
  424.5 68.4 %collective-permute-start.31 = (f32[8,256,128]{2,1,0:T(8,128)}, f32[8,256,128]{2,1,0:T(8,128)}, u32[]{:S(2)}, u32[]{:S(2)}) collective-permute-start(f32[8,256,128]{2,1,0:T(8,128)} %get-tuple-element.124), channel_id=1, source_target_pairs={{0,16},{8,24},{16,0},{24,8},{1,17},{9,25},{17,1},{25,9},{2,18},{10... | collective-permute-start | bytes 3145736 | tf_op jit(solution)/shard_map/ppermute | solution.py:419
  425.0 89.3 %collective-permute-start.32 = (f32[8,256,128]{2,1,0:T(8,128)}, f32[8,256,128]{2,1,0:T(8,128)}, u32[]{:S(2)}, u32[]{:S(2)}) collective-permute-start(f32[8,256,128]{2,1,0:T(8,128)} %get-tuple-element.125), channel_id=1, source_target_pairs={{0,24},{8,16},{16,8},{24,0},{1,25},{9,17},{17,9},{25,1},{2,26},{10... | collective-permute-start | bytes 3145736 | tf_op jit(solution)/shard_map/ppermute | solution.py:419
  426.6 175.6 %all-to-all-start.2 = ((f32[64,8,16,128]{3,2,1,0:T(8,128)}), f32[64,8,16,128]{3,2,1,0:T(8,128)}, u32[]{:S(2)}, u32[]{:S(2)}) async-start(f32[64,8,16,128]{3,2,1,0:T(8,128)} %shard_map.89), calls=%async_computation.2 | async-start | bytes 8388608 | tf_op jit(solution)/shard_map/all_to_all | solution.py:514
  486.3 72.9 %copy-start.15 = (f32[8,256,128]{2,1,0:T(8,128)}, f32[8,256,128]{2,1,0:T(8,128)S(1)}, u32[]{:S(2)}) copy-start(f32[8,256,128]{2,1,0:T(8,128)S(1)} %get-tuple-element.119.refs_0_.refs_5_) | copy-start | bytes 3145732
  486.3 28.6 %collective-permute-start.27 = (f32[8,256,128]{2,1,0:T(8,128)S(1)}, f32[8,256,128]{2,1,0:T(8,128)S(1)}, u32[]{:S(2)}, u32[]{:S(2)}) collective-permute-start(f32[8,256,128]{2,1,0:T(8,128)S(1)} %get-tuple-element.120), channel_id=1, source_target_pairs={{0,8},{8,0},{16,24},{24,16},{1,9},{9,1},{17,25},{25,17},{2,10},{10... | collective-permute-start | bytes 3145736 | tf_op jit(solution)/shard_map/ppermute | solution.py:419
  487.5 75.2 %collective-permute-start.18 = (f32[8,256,128]{2,1,0:T(8,128)S(1)}, f32[8,256,128]{2,1,0:T(8,128)}, u32[]{:S(2)}, u32[]{:S(2)}) collective-permute-start(f32[8,256,128]{2,1,0:T(8,128)S(1)} %copy-done.23), channel_id=1, source_target_pairs={{0,8},{8,0},{16,24},{24,16},{1,9},{9,1},{17,25},{25,17},{2,10},{10... | collective-permute-start | bytes 3145736 | tf_op jit(solution)/shard_map/ppermute | solution.py:419
  487.6 50.2 %collective-permute-start.28 = (f32[8,256,128]{2,1,0:T(8,128)S(1)}, f32[8,256,128]{2,1,0:T(8,128)S(1)}, u32[]{:S(2)}, u32[]{:S(2)}) collective-permute-start(f32[8,256,128]{2,1,0:T(8,128)S(1)} %get-tuple-element.121), channel_id=1, source_target_pairs={{0,16},{8,24},{16,0},{24,8},{1,17},{9,25},{17,1},{25,9},{2,18},{10... | collective-permute-start | bytes 3145736 | tf_op jit(solution)/shard_map/ppermute | solution.py:419
  492.9 66.3 %collective-permute-start.29 = (f32[8,256,128]{2,1,0:T(8,128)S(1)}, f32[8,256,128]{2,1,0:T(8,128)S(1)}, u32[]{:S(2)}, u32[]{:S(2)}) collective-permute-start(f32[8,256,128]{2,1,0:T(8,128)S(1)} %get-tuple-element.122), channel_id=1, source_target_pairs={{0,24},{8,16},{16,8},{24,0},{1,25},{9,17},{17,9},{25,1},{2,26},{10... | collective-permute-start | bytes 3145736 | tf_op jit(solution)/shard_map/ppermute | solution.py:419
  514.4 68.4 %collective-permute-start.19 = (f32[8,256,128]{2,1,0:T(8,128)S(1)}, f32[8,256,128]{2,1,0:T(8,128)}, u32[]{:S(2)}, u32[]{:S(2)}) collective-permute-start(f32[8,256,128]{2,1,0:T(8,128)S(1)} %copy-done.21), channel_id=1, source_target_pairs={{0,16},{8,24},{16,0},{24,8},{1,17},{9,25},{17,1},{25,9},{2,18},{10... | collective-permute-start | bytes 3145736 | tf_op jit(solution)/shard_map/ppermute | solution.py:419
  514.9 87.3 %collective-permute-start.20 = (f32[8,256,128]{2,1,0:T(8,128)S(1)}, f32[8,256,128]{2,1,0:T(8,128)}, u32[]{:S(2)}, u32[]{:S(2)}) collective-permute-start(f32[8,256,128]{2,1,0:T(8,128)S(1)} %copy-done.19), channel_id=1, source_target_pairs={{0,24},{8,16},{16,8},{24,0},{1,25},{9,17},{17,9},{25,1},{2,26},{10... | collective-permute-start | bytes 3145736 | tf_op jit(solution)/shard_map/ppermute | solution.py:419
  618.9 3.3 collective-permute-start.33
  619.9 26.0 %collective-permute-start.34 = (f32[8,256,128]{2,1,0:T(8,128)S(1)}, f32[8,256,128]{2,1,0:T(8,128)S(1)}, u32[]{:S(2)}, u32[]{:S(2)}) collective-permute-start(f32[8,256,128]{2,1,0:T(8,128)S(1)} %get-tuple-element.128), channel_id=1, source_target_pairs={{0,16},{8,24},{16,0},{24,8},{1,17},{9,25},{17,1},{25,9},{2,18},{10... | collective-permute-start | bytes 3145736 | tf_op jit(solution)/shard_map/ppermute | solution.py:419
  621.4 45.2 %collective-permute-start.35 = (f32[8,256,128]{2,1,0:T(8,128)S(1)}, f32[8,256,128]{2,1,0:T(8,128)S(1)}, u32[]{:S(2)}, u32[]{:S(2)}) collective-permute-start(f32[8,256,128]{2,1,0:T(8,128)S(1)} %get-tuple-element.129), channel_id=1, source_target_pairs={{0,24},{8,16},{16,8},{24,0},{1,25},{9,17},{17,9},{25,1},{2,26},{10... | collective-permute-start | bytes 3145736 | tf_op jit(solution)/shard_map/ppermute | solution.py:419
  667.5 1.5 collective-permute-start.36
  669.0 3.6 collective-permute-start.37
  672.6 3.6 collective-permute-start.38
  676.2 4.5 collective-permute-start.39
  680.7 5.0 collective-permute-start.40
  (37 other events, 448.5 us)
